TPU v7x, 256 devices: a whole 4x4x8 slice. The times are simulated.
256 devices in a mesh: section: 16 (over z, core), dp: 16 (over x, y).
Axes of the slice: x: 4, y: 4, z: 8, core: 2. Of those that a mesh axis runs over, the one named last changes fastest.
Arguments:
- tokens: bfloat16 [16, 192, 4096], P('dp'), may hold values from -6 to 6
- upstream: bfloat16 [16, 192, 4096], P('dp'), may hold values from -6 to 6
- gains: bfloat16 [16, 4096], P('section'), may hold values from 0.5 to 1.5
- w_kv: bfloat16 [16, 4096, 1024], P('section'), may hold values from -0.09375 to 0.09375
- doc_lengths: int32 [16, 4], P('dp'), may hold values from 1 to 96, 192 in all within a row
- seg_lengths: int32 [16, 4], P('dp'), may hold values from 1 to 60, 192 in all within a row
- block_mask: int32 [16, 12, 12], P('dp'), may hold values 0 or 1
Outputs:
- grad_kv: float32 [16, 4096, 1024], P('section', 'dp')
- grad_gain: float32 [16, 4096], P('section', 'dp')
Inputs may be any that keep to these rules, and one draw needn't show every extreme that they name: `doc_lengths`: each row sums to 192. `seg_lengths`: each row sums to 192.
All inputs are finite; a program needn't handle non-finite values. No bound on the sum of `block_mask` on one device may be relied on, other than what follows from the above.
Results may differ from a plain program's by a relative error of at most 0.035.
Values may be sent and summed in bfloat16 or wider, within the bound.
A program may use at most 128 MiB of HBM per device.

v0:
```python
import jax
import jax.numpy as jnp
from jax import lax
from jax.sharding import PartitionSpec as P

HEADS = 32
KV_HEADS = 4
HEAD_DIM = 128
SEGS = 4
BLK = 16
SEGMAX = 60


EPSILON = 1e-06


def from_behind(block, axis, distance):
    devices = range(lax.axis_size(axis))
    route = [(i - distance, i) for i in devices if i - distance in devices]
    return lax.ppermute(block, axis, route)


def local(tokens, upstream, gains, w_kv, doc_lengths, seg_lengths, block_mask):
    section_count = lax.axis_size("section")
    section_id = lax.axis_index("section")
    inputs_all = tokens[0]
    seq_len = inputs_all.shape[0]
    width = inputs_all.shape[1]
    weight = w_kv[0]
    kv_width = weight.shape[1] // 2
    gain_row = gains[0].astype(jnp.float32)
    scale = HEAD_DIM ** (-0.5)
    group_size = HEADS // KV_HEADS
    positions = jnp.arange(seq_len, dtype=jnp.int32)
    doc_ends = jnp.cumsum(doc_lengths[0])
    doc_ids = jnp.sum((positions[:, None] >= doc_ends[None, :]).astype(jnp.int32), 1)
    seg_counts = seg_lengths[0]
    seg_ends = jnp.cumsum(seg_counts)
    seg_ids = jnp.sum((positions[:, None] >= seg_ends[None, :]).astype(jnp.int32), 1)
    seg_sizes = jnp.sum(
        jnp.where(seg_ids[:, None] == jnp.arange(SEGS)[None, :], seg_counts[None, :], 0), 1
    )
    blocks = seq_len // BLK
    key_blocks = positions // BLK
    key_select = (jnp.arange(blocks)[:, None] == key_blocks[None, :]).astype(jnp.float32)
    table = block_mask[0].astype(jnp.float32)
    window = SEGMAX
    starts = seg_ends - seg_counts
    padded = seq_len + window
    doc_padded = jnp.concatenate([doc_ids, jnp.full((window,), -1, jnp.int32)])
    offsets = jnp.arange(window, dtype=jnp.int32)

    def allowed_keys(start):
        query_rows = start + offsets
        query_docs = lax.dynamic_slice_in_dim(doc_padded, start, window, 0)
        query_blocks = jnp.minimum(query_rows // BLK, blocks - 1)
        row_select = (query_blocks[:, None] == jnp.arange(blocks)[None, :]).astype(jnp.float32)
        block_open = jnp.dot(jnp.dot(row_select, table), key_select) > 0.5
        same_block = query_blocks[:, None] == key_blocks[None, :]
        causal = positions[None, :] <= query_rows[:, None]
        return causal & (query_docs[:, None] == doc_ids[None, :]) & (block_open | same_block)

    def normalize(inputs_win):
        values = inputs_win.astype(jnp.float32)
        inverse = lax.rsqrt(jnp.mean(values * values, -1, keepdims=True) + EPSILON)
        return (values, inverse, values * inverse)

    def masked_write(buffer, block_rows, start, live):
        former = lax.dynamic_slice_in_dim(buffer, start, window, 0)
        fresh = jnp.where(live[:, None], block_rows, former)
        return lax.dynamic_update_slice_in_dim(buffer, fresh, start, 0)

    def attention_probs(hidden_win, key_values, allowed, live):
        query = hidden_win.reshape(window, KV_HEADS, group_size, HEAD_DIM)
        key_part = key_values[:seq_len, :kv_width].reshape(seq_len, KV_HEADS, HEAD_DIM)
        value_part = key_values[:seq_len, kv_width:].reshape(seq_len, KV_HEADS, HEAD_DIM)
        scores = (
            jnp.einsum("ikgd,jkd->kgij", query, key_part, preferred_element_type=jnp.float32)
            * scale
        )
        raw_probs = jnp.where(allowed[None, None], jnp.exp(scores), 0.0)
        totals = jnp.sum(raw_probs, -1, keepdims=True)
        totals = jnp.where(live[None, None, :, None], totals, 1.0)
        probs = raw_probs / totals
        return (query, key_part, value_part, probs, probs.astype(jnp.bfloat16))

    def forward_piece(inputs_win, start, count, x_buf, h_buf, kv_buf):
        live = offsets < count
        values, inverse, normed = normalize(inputs_win)
        hidden_win = (normed * gain_row).astype(jnp.bfloat16)
        kv_win = jnp.dot(hidden_win, weight, preferred_element_type=jnp.float32).astype(
            jnp.bfloat16
        )
        x_buf = masked_write(x_buf, inputs_win, start, live)
        h_buf = masked_write(h_buf, hidden_win, start, live)
        kv_buf = masked_write(kv_buf, kv_win, start, live)
        allowed = allowed_keys(start)
        query, key_part, value_part, probs, probs_low = attention_probs(
            hidden_win, kv_buf, allowed, live
        )
        mixed = jnp.einsum(
            "kgij,jkd->ikgd", probs_low, value_part, preferred_element_type=jnp.float32
        ).reshape(window, width)
        return ((values + mixed).astype(jnp.bfloat16), x_buf, h_buf, kv_buf)

    inputs_padded = jnp.concatenate([inputs_all, jnp.zeros((window, width), jnp.bfloat16)])
    steps = SEGS + section_count - 1

    def forward_step(step_id, carry):
        inbox, x_buf, h_buf, kv_buf = carry
        piece_id = step_id - section_id
        active_now = (piece_id >= 0) & (piece_id < SEGS)
        clipped = jnp.clip(piece_id, 0, SEGS - 1)
        start = starts[clipped]
        count = seg_counts[clipped]
        first_rows = lax.dynamic_slice_in_dim(inputs_padded, start, window, 0)
        inputs_win = jnp.where(section_id == 0, first_rows, inbox)

        def forward_working(operand):
            return forward_piece(inputs_win, start, count, x_buf, h_buf, kv_buf)

        def forward_resting(operand):
            return (jnp.zeros_like(inbox), x_buf, h_buf, kv_buf)

        outgoing, x_buf, h_buf, kv_buf = lax.cond(active_now, forward_working, forward_resting, 0)
        inbox = from_behind(outgoing, "section", 1)
        return (inbox, x_buf, h_buf, kv_buf)

    forward_init = (
        jnp.zeros((window, width), jnp.bfloat16),
        jnp.zeros((padded, width), jnp.bfloat16),
        jnp.zeros((padded, width), jnp.bfloat16),
        jnp.zeros((padded, 2 * kv_width), jnp.bfloat16),
    )
    unused_inbox, x_buf, h_buf, kv_buf = lax.fori_loop(0, steps, forward_step, forward_init)
    factor = seq_len / (SEGS * seg_sizes.astype(jnp.float32))
    start_grads = (upstream[0].astype(jnp.float32) * factor[:, None]).astype(jnp.bfloat16)
    grads_padded = jnp.concatenate([start_grads, jnp.zeros((window, width), jnp.bfloat16)])

    def backward_piece(grads_in, start, count, key_acc, dkv_buf, gain_sum):
        live = offsets < count
        grads_in = jnp.where(live[:, None], grads_in, jnp.zeros_like(grads_in))
        inputs_win = lax.dynamic_slice_in_dim(x_buf, start, window, 0)
        values, inverse, normed = normalize(inputs_win)
        hidden_win = lax.dynamic_slice_in_dim(h_buf, start, window, 0)
        allowed = allowed_keys(start)
        query, key_part, value_part, probs, probs_low = attention_probs(
            hidden_win, kv_buf, allowed, live
        )
        grad_out = grads_in.reshape(window, KV_HEADS, group_size, HEAD_DIM)
        d_probs = jnp.einsum(
            "ikgd,jkd->kgij", grad_out, value_part, preferred_element_type=jnp.float32
        )
        d_scores = probs * (d_probs - jnp.sum(probs * d_probs, -1, keepdims=True))
        d_low = (d_scores * scale).astype(jnp.bfloat16)
        d_query = jnp.einsum(
            "kgij,jkd->ikgd", d_low, key_part, preferred_element_type=jnp.float32
        ).reshape(window, width)
        d_keys = jnp.einsum(
            "kgij,ikgd->jkd", d_low, query, preferred_element_type=jnp.float32
        ).reshape(seq_len, kv_width)
        d_values = jnp.einsum(
            "kgij,ikgd->jkd", probs_low, grad_out, preferred_element_type=jnp.float32
        ).reshape(seq_len, kv_width)
        key_acc = key_acc.at[:seq_len].add(jnp.concatenate([d_keys, d_values], 1))
        d_kv = jnp.where(
            live[:, None], lax.dynamic_slice_in_dim(key_acc, start, window, 0), 0.0
        ).astype(jnp.bfloat16)
        dkv_buf = masked_write(dkv_buf, d_kv, start, live)
        d_hidden = d_query + lax.dot_general(
            d_kv, weight, (((1,), (1,)), ((), ())), preferred_element_type=jnp.float32
        )
        gain_sum = gain_sum + jnp.sum(d_hidden * normed, 0)
        d_normed = d_hidden * gain_row
        d_inputs = inverse * (d_normed - normed * jnp.mean(d_normed * normed, -1, keepdims=True))
        grads_out = jnp.where(live[:, None], grads_in.astype(jnp.float32) + d_inputs, 0.0).astype(
            jnp.bfloat16
        )
        return (grads_out, key_acc, dkv_buf, gain_sum)

    def backward_step(step_id, carry):
        inbox, key_acc, dkv_buf, gain_sum = carry
        turn = step_id - (section_count - 1 - section_id)
        active_now = (turn >= 0) & (turn < SEGS)
        clipped = jnp.clip(SEGS - 1 - turn, 0, SEGS - 1)
        start = starts[clipped]
        count = seg_counts[clipped]
        last_rows = lax.dynamic_slice_in_dim(grads_padded, start, window, 0)
        grads_in = jnp.where(section_id == section_count - 1, last_rows, inbox)

        def backward_working(operand):
            return backward_piece(grads_in, start, count, key_acc, dkv_buf, gain_sum)

        def backward_resting(operand):
            return (jnp.zeros_like(inbox), key_acc, dkv_buf, gain_sum)

        outgoing, key_acc, dkv_buf, gain_sum = lax.cond(
            active_now, backward_working, backward_resting, 0
        )
        inbox = from_behind(outgoing, "section", -1)
        return (inbox, key_acc, dkv_buf, gain_sum)

    backward_init = (
        jnp.zeros((window, width), jnp.bfloat16),
        jnp.zeros((padded, 2 * kv_width), jnp.float32),
        jnp.zeros((padded, 2 * kv_width), jnp.bfloat16),
        jnp.zeros((width,), jnp.float32),
    )
    unused_grads, key_acc, dkv_buf, gain_sum = lax.fori_loop(0, steps, backward_step, backward_init)
    hidden_all = h_buf[:seq_len]
    dkv_all = dkv_buf[:seq_len]
    local_grads = lax.dot_general(
        hidden_all, dkv_all, (((0,), (0,)), ((), ())), preferred_element_type=jnp.float32
    )
    grad_weight, grad_gain = (
        lax.psum_scatter(
            local_grads.astype(jnp.bfloat16), "dp", scatter_dimension=0, tiled=True
        ).astype(jnp.float32),
        lax.psum_scatter(
            gain_sum.astype(jnp.bfloat16), "dp", scatter_dimension=0, tiled=True
        ).astype(jnp.float32),
    )
    return (grad_weight[None], grad_gain[None])


def solution(mesh):
    placed = (
        P("dp", None, None),
        P("dp", None, None),
        P("section", None),
        P("section", None, None),
        P("dp", None),
        P("dp", None),
        P("dp", None, None),
    )
    return jax.shard_map(
        local,
        mesh=mesh,
        in_specs=placed,
        out_specs=(P("section", "dp", None), P("section", "dp")),
        check_vma=False,
    )
```

profile of v0, /device:TPU:2, one launch (start us, length us, event | category | flops | bytes accessed | tf_op | source)
XLA Modules:
  0.0 2003.5 jit_solution(17396073797739822887)
XLA Ops:
  23.1 640.9 %while.46 = (s32[]{:T(128)}, bf16[60,4096]{1,0:T(8,128)(2,1)S(1)}, bf16[252,4096]{1,0:T(8,128)(2,1)S(1)}, bf16[252,4096]{1,0:T(8,128)(2,1)}, bf16[252,1024]{1,0:...) while((s32[]{:T(128)}, bf16[60,4096]{1,0:T(8,128)(2,1)S(1)}, ...), condition=%wide.region_8.9_spmd.clone.clone, body=%wide.region_3.8_spmd.clone.clone.sunk | while | flops 698340800 | bytes 37559312 | solution.py:135
  25.5 37.1 %conditional.8 = (bf16[60,4096]{1,0:T(8,128)(2,1)}, bf16[252,4096]{1,0:T(8,128)(2,1)S(1)}, bf16[252,4096]{1,0:T(8,128)(2,1)}, bf16[252,1024]{1,0:T(8,128)(2,1)}) conditional(s32[]{:T(128)} %convert_element_type.239, (bf16[252,4096]{1,0:T(8,128)(2,1)S(1)}, bf16[252,4096]{1,0:T(8,128)(2,1)}, bf16[252,1024]{1,0:T(8,128)(2,1)}) %tuple.155, ...), branch_computations={%region_4.4_spmd, %region_5.7_spmd.clone} | conditional | flops 698336000 | bytes 35585612 | solution.py:125
  35.3 5.0 fusion.17
  55.7 4.1 dynamic_update_slice.26
  68.1 37.1 %conditional.8 = (bf16[60,4096]{1,0:T(8,128)(2,1)}, bf16[252,4096]{1,0:T(8,128)(2,1)S(1)}, bf16[252,4096]{1,0:T(8,128)(2,1)}, bf16[252,1024]{1,0:T(8,128)(2,1)}) conditional(s32[]{:T(128)} %convert_element_type.239, (bf16[252,4096]{1,0:T(8,128)(2,1)S(1)}, bf16[252,4096]{1,0:T(8,128)(2,1)}, bf16[252,1024]{1,0:T(8,128)(2,1)}) %tuple.155, ...), branch_computations={%region_4.4_spmd, %region_5.7_spmd.clone} | conditional | flops 698336000 | bytes 35585612 | solution.py:125
  77.9 5.0 fusion.17
  98.3 4.1 dynamic_update_slice.26
  111.7 37.1 %conditional.8 = (bf16[60,4096]{1,0:T(8,128)(2,1)}, bf16[252,4096]{1,0:T(8,128)(2,1)S(1)}, bf16[252,4096]{1,0:T(8,128)(2,1)}, bf16[252,1024]{1,0:T(8,128)(2,1)}) conditional(s32[]{:T(128)} %convert_element_type.239, (bf16[252,4096]{1,0:T(8,128)(2,1)S(1)}, bf16[252,4096]{1,0:T(8,128)(2,1)}, bf16[252,1024]{1,0:T(8,128)(2,1)}) %tuple.155, ...), branch_computations={%region_4.4_spmd, %region_5.7_spmd.clone} | conditional | flops 698336000 | bytes 35585612 | solution.py:125
  121.5 5.0 fusion.17
  141.9 4.1 dynamic_update_slice.26
  148.8 6.6 collective-permute-start
  159.6 37.1 %conditional.8 = (bf16[60,4096]{1,0:T(8,128)(2,1)}, bf16[252,4096]{1,0:T(8,128)(2,1)S(1)}, bf16[252,4096]{1,0:T(8,128)(2,1)}, bf16[252,1024]{1,0:T(8,128)(2,1)}) conditional(s32[]{:T(128)} %convert_element_type.239, (bf16[252,4096]{1,0:T(8,128)(2,1)S(1)}, bf16[252,4096]{1,0:T(8,128)(2,1)}, bf16[252,1024]{1,0:T(8,128)(2,1)}) %tuple.155, ...), branch_computations={%region_4.4_spmd, %region_5.7_spmd.clone} | conditional | flops 698336000 | bytes 35585612 | solution.py:125
  169.4 5.0 fusion.17
  189.8 4.1 dynamic_update_slice.26
  196.7 9.0 collective-permute-start
  210.7 45.3 %collective-permute-start = (bf16[60,4096]{1,0:T(8,128)(2,1)}, bf16[60,4096]{1,0:T(8,128)(2,1)S(1)}, u32[]{:S(2)}, u32[]{:S(2)}) collective-permute-start(bf16[60,4096]{1,0:T(8,128)(2,1)} %get-tuple-element.1957), channel_id=1, source_target_pairs={{0,16},{16,32},{32,48},{48,64},{64,80},{80,96},{96,112},{112,128},... | collective-permute-start | bytes 1474568 | tf_op jit(solution)/shard_map/while/body/eval_jaxpr/ppermute | solution.py:20
  261.0 9.0 collective-permute-start
  275.0 45.3 %collective-permute-start = (bf16[60,4096]{1,0:T(8,128)(2,1)}, bf16[60,4096]{1,0:T(8,128)(2,1)S(1)}, u32[]{:S(2)}, u32[]{:S(2)}) collective-permute-start(bf16[60,4096]{1,0:T(8,128)(2,1)} %get-tuple-element.1957), channel_id=1, source_target_pairs={{0,16},{16,32},{32,48},{48,64},{64,80},{80,96},{96,112},{112,128},... | collective-permute-start | bytes 1474568 | tf_op jit(solution)/shard_map/while/body/eval_jaxpr/ppermute | solution.py:20
  325.2 9.0 collective-permute-start
  339.2 31.5 %collective-permute-start = (bf16[60,4096]{1,0:T(8,128)(2,1)}, bf16[60,4096]{1,0:T(8,128)(2,1)S(1)}, u32[]{:S(2)}, u32[]{:S(2)}) collective-permute-start(bf16[60,4096]{1,0:T(8,128)(2,1)} %get-tuple-element.1957), channel_id=1, source_target_pairs={{0,16},{16,32},{32,48},{48,64},{64,80},{80,96},{96,112},{112,128},... | collective-permute-start | bytes 1474568 | tf_op jit(solution)/shard_map/while/body/eval_jaxpr/ppermute | solution.py:20
  375.7 9.0 collective-permute-start
  389.7 42.9 %collective-permute-start = (bf16[60,4096]{1,0:T(8,128)(2,1)}, bf16[60,4096]{1,0:T(8,128)(2,1)S(1)}, u32[]{:S(2)}, u32[]{:S(2)}) collective-permute-start(bf16[60,4096]{1,0:T(8,128)(2,1)} %get-tuple-element.1957), channel_id=1, source_target_pairs={{0,16},{16,32},{32,48},{48,64},{64,80},{80,96},{96,112},{112,128},... | collective-permute-start | bytes 1474568 | tf_op jit(solution)/shard_map/while/body/eval_jaxpr/ppermute | solution.py:20
  437.6 9.0 collective-permute-start
  451.6 31.5 %collective-permute-start = (bf16[60,4096]{1,0:T(8,128)(2,1)}, bf16[60,4096]{1,0:T(8,128)(2,1)S(1)}, u32[]{:S(2)}, u32[]{:S(2)}) collective-permute-start(bf16[60,4096]{1,0:T(8,128)(2,1)} %get-tuple-element.1957), channel_id=1, source_target_pairs={{0,16},{16,32},{32,48},{48,64},{64,80},{80,96},{96,112},{112,128},... | collective-permute-start | bytes 1474568 | tf_op jit(solution)/shard_map/while/body/eval_jaxpr/ppermute | solution.py:20
  488.1 9.0 collective-permute-start
  502.1 42.9 %collective-permute-start = (bf16[60,4096]{1,0:T(8,128)(2,1)}, bf16[60,4096]{1,0:T(8,128)(2,1)S(1)}, u32[]{:S(2)}, u32[]{:S(2)}) collective-permute-start(bf16[60,4096]{1,0:T(8,128)(2,1)} %get-tuple-element.1957), channel_id=1, source_target_pairs={{0,16},{16,32},{32,48},{48,64},{64,80},{80,96},{96,112},{112,128},... | collective-permute-start | bytes 1474568 | tf_op jit(solution)/shard_map/while/body/eval_jaxpr/ppermute | solution.py:20
  550.0 9.0 collective-permute-start
  564.0 31.6 %collective-permute-start = (bf16[60,4096]{1,0:T(8,128)(2,1)}, bf16[60,4096]{1,0:T(8,128)(2,1)S(1)}, u32[]{:S(2)}, u32[]{:S(2)}) collective-permute-start(bf16[60,4096]{1,0:T(8,128)(2,1)} %get-tuple-element.1957), channel_id=1, source_target_pairs={{0,16},{16,32},{32,48},{48,64},{64,80},{80,96},{96,112},{112,128},... | collective-permute-start | bytes 1474568 | tf_op jit(solution)/shard_map/while/body/eval_jaxpr/ppermute | solution.py:20
  600.6 10.2 collective-permute-start
  615.8 46.5 %collective-permute-start = (bf16[60,4096]{1,0:T(8,128)(2,1)}, bf16[60,4096]{1,0:T(8,128)(2,1)S(1)}, u32[]{:S(2)}, u32[]{:S(2)}) collective-permute-start(bf16[60,4096]{1,0:T(8,128)(2,1)} %get-tuple-element.1957), channel_id=1, source_target_pairs={{0,16},{16,32},{32,48},{48,64},{64,80},{80,96},{96,112},{112,128},... | collective-permute-start | bytes 1474568 | tf_op jit(solution)/shard_map/while/body/eval_jaxpr/ppermute | solution.py:20
  666.6 1234.5 %while.47 = (s32[]{:T(128)}, bf16[60,4096]{1,0:T(8,128)(2,1)S(1)}, f32[252,1024]{1,0:T(8,128)}, bf16[252,1024]{1,0:T(8,128)(2,1)}, f32[4096]{0:T(1024)}, /*index...) while((s32[]{:T(128)}, bf16[60,4096]{1,0:T(8,128)(2,1)S(1)}, ...), condition=%wide.region_19.20_spmd.clone.clone, body=%wide.region_11.19_spmd.clone.clone.sunk | while | flops 988425728 | bytes 90528624 | solution.py:209
  669.5 10.5 collective-permute-done.1
  682.8 31.4 %collective-permute-done.1 = bf16[60,4096]{1,0:T(8,128)(2,1)S(1)} collective-permute-done((bf16[60,4096]{1,0:T(8,128)(2,1)}, bf16[60,4096]{1,0:T(8,128)(2,1)S(1)}, u32[]{:S(2)}, u32[]{:S(2)}) %collective-permute-start.1) | collective-permute-done | bytes 491552 | tf_op jit(solution)/shard_map/while/body/eval_jaxpr/ppermute | solution.py:20
  717.1 10.5 collective-permute-done.1
  730.4 42.8 %collective-permute-done.1 = bf16[60,4096]{1,0:T(8,128)(2,1)S(1)} collective-permute-done((bf16[60,4096]{1,0:T(8,128)(2,1)}, bf16[60,4096]{1,0:T(8,128)(2,1)S(1)}, u32[]{:S(2)}, u32[]{:S(2)}) %collective-permute-start.1) | collective-permute-done | bytes 491552 | tf_op jit(solution)/shard_map/while/body/eval_jaxpr/ppermute | solution.py:20
  776.1 10.5 collective-permute-done.1
  789.4 31.4 %collective-permute-done.1 = bf16[60,4096]{1,0:T(8,128)(2,1)S(1)} collective-permute-done((bf16[60,4096]{1,0:T(8,128)(2,1)}, bf16[60,4096]{1,0:T(8,128)(2,1)S(1)}, u32[]{:S(2)}, u32[]{:S(2)}) %collective-permute-start.1) | collective-permute-done | bytes 491552 | tf_op jit(solution)/shard_map/while/body/eval_jaxpr/ppermute | solution.py:20
  823.7 10.5 collective-permute-done.1
  837.0 42.8 %collective-permute-done.1 = bf16[60,4096]{1,0:T(8,128)(2,1)S(1)} collective-permute-done((bf16[60,4096]{1,0:T(8,128)(2,1)}, bf16[60,4096]{1,0:T(8,128)(2,1)S(1)}, u32[]{:S(2)}, u32[]{:S(2)}) %collective-permute-start.1) | collective-permute-done | bytes 491552 | tf_op jit(solution)/shard_map/while/body/eval_jaxpr/ppermute | solution.py:20
  882.7 10.6 collective-permute-done.1
  896.1 31.3 %collective-permute-done.1 = bf16[60,4096]{1,0:T(8,128)(2,1)S(1)} collective-permute-done((bf16[60,4096]{1,0:T(8,128)(2,1)}, bf16[60,4096]{1,0:T(8,128)(2,1)S(1)}, u32[]{:S(2)}, u32[]{:S(2)}) %collective-permute-start.1) | collective-permute-done | bytes 491552 | tf_op jit(solution)/shard_map/while/body/eval_jaxpr/ppermute | solution.py:20
  930.3 10.6 collective-permute-done.1
  943.7 42.6 %collective-permute-done.1 = bf16[60,4096]{1,0:T(8,128)(2,1)S(1)} collective-permute-done((bf16[60,4096]{1,0:T(8,128)(2,1)}, bf16[60,4096]{1,0:T(8,128)(2,1)S(1)}, u32[]{:S(2)}, u32[]{:S(2)}) %collective-permute-start.1) | collective-permute-done | bytes 491552 | tf_op jit(solution)/shard_map/while/body/eval_jaxpr/ppermute | solution.py:20
  989.3 10.6 collective-permute-done.1
  1002.7 31.3 %collective-permute-done.1 = bf16[60,4096]{1,0:T(8,128)(2,1)S(1)} collective-permute-done((bf16[60,4096]{1,0:T(8,128)(2,1)}, bf16[60,4096]{1,0:T(8,128)(2,1)S(1)}, u32[]{:S(2)}, u32[]{:S(2)}) %collective-permute-start.1) | collective-permute-done | bytes 491552 | tf_op jit(solution)/shard_map/while/body/eval_jaxpr/ppermute | solution.py:20
  1036.9 646.3 %collective-permute-done.1 = bf16[60,4096]{1,0:T(8,128)(2,1)S(1)} collective-permute-done((bf16[60,4096]{1,0:T(8,128)(2,1)}, bf16[60,4096]{1,0:T(8,128)(2,1)S(1)}, u32[]{:S(2)}, u32[]{:S(2)}) %collective-permute-start.1) | collective-permute-done | bytes 491552 | tf_op jit(solution)/shard_map/while/body/eval_jaxpr/ppermute | solution.py:20
  1683.8 43.9 %conditional.9 = (bf16[60,4096]{1,0:T(8,128)(2,1)}, f32[252,1024]{1,0:T(8,128)}, bf16[252,1024]{1,0:T(8,128)(2,1)}, f32[4096]{0:T(1024)}) conditional(s32[]{:T(128)} %convert_element_type.241, (f32[252,1024]{1,0:T(8,128)}, bf16[252,1024]{1,0:T(8,128)(2,1)}, f32[4096]{0:T(1024)}) %tuple.158, (s32[]{:T(128)}, s32[4]{0:T(128)}, ...), branch_computations={%region_12.12_spmd, %region_13.18_spmd.clone} | conditional | flops 988420928 | bytes 88554880 | solution.py:197
  1703.0 10.5 fusion.41
  1718.3 3.8 fusion.55
  1729.0 10.8 collective-permute-done.1
  1740.5 43.9 %conditional.9 = (bf16[60,4096]{1,0:T(8,128)(2,1)}, f32[252,1024]{1,0:T(8,128)}, bf16[252,1024]{1,0:T(8,128)(2,1)}, f32[4096]{0:T(1024)}) conditional(s32[]{:T(128)} %convert_element_type.241, (f32[252,1024]{1,0:T(8,128)}, bf16[252,1024]{1,0:T(8,128)(2,1)}, f32[4096]{0:T(1024)}) %tuple.158, (s32[]{:T(128)}, s32[4]{0:T(128)}, ...), branch_computations={%region_12.12_spmd, %region_13.18_spmd.clone} | conditional | flops 988420928 | bytes 88554880 | solution.py:197
  1759.6 10.5 fusion.41
  1774.9 3.8 fusion.55
  1785.6 10.5 collective-permute-done.1
  1796.8 43.9 %conditional.9 = (bf16[60,4096]{1,0:T(8,128)(2,1)}, f32[252,1024]{1,0:T(8,128)}, bf16[252,1024]{1,0:T(8,128)(2,1)}, f32[4096]{0:T(1024)}) conditional(s32[]{:T(128)} %convert_element_type.241, (f32[252,1024]{1,0:T(8,128)}, bf16[252,1024]{1,0:T(8,128)(2,1)}, f32[4096]{0:T(1024)}) %tuple.158, (s32[]{:T(128)}, s32[4]{0:T(128)}, ...), branch_computations={%region_12.12_spmd, %region_13.18_spmd.clone} | conditional | flops 988420928 | bytes 88554880 | solution.py:197
  1816.0 10.5 fusion.41
  1831.3 3.8 fusion.55
  1842.0 10.6 collective-permute-done.1
  1853.3 43.9 %conditional.9 = (bf16[60,4096]{1,0:T(8,128)(2,1)}, f32[252,1024]{1,0:T(8,128)}, bf16[252,1024]{1,0:T(8,128)(2,1)}, f32[4096]{0:T(1024)}) conditional(s32[]{:T(128)} %convert_element_type.241, (f32[252,1024]{1,0:T(8,128)}, bf16[252,1024]{1,0:T(8,128)(2,1)}, f32[4096]{0:T(1024)}) %tuple.158, (s32[]{:T(128)}, s32[4]{0:T(128)}, ...), branch_computations={%region_12.12_spmd, %region_13.18_spmd.clone} | conditional | flops 988420928 | bytes 88554880 | solution.py:197
  1872.4 10.5 fusion.41
  1887.7 3.8 fusion.55
  1901.1 7.1 convolution_convert_fusion.1
  1910.2 35.6 %all-reduce.3 = bf16[4096]{0:T(1024)(128)(2,1)S(1)} all-reduce(bf16[4096]{0:T(1024)(128)(2,1)S(1)} %convert_element_type.144), channel_id=3, replica_groups=mesh['section'=16,'dp'=16] {'dp'}, use_global_device_ids=true, to_apply=%region_21.22.clone | all-reduce | flops 4096 | bytes 16384
  1946.4 48.1 %reduce-scatter.2.cloned.1.call-done = bf16[256,1024]{1,0:T(8,128)(2,1)} async-done(((bf16[4096,1024]{1,0:T(8,128)(2,1)}), bf16[256,1024]{1,0:T(8,128)(2,1)}) %reduce-scatter.2.cloned.1.call-update) | async-done | bytes 524304 | tf_op jit(solution)/shard_map/reduce_scatter | solution.py:216
  (677 shorter events, 408.4 us)
Async XLA Ops:
  7.2 1987.4 %reduce-scatter.2.cloned.1.call-start = ((), (), s32[]{:S(2)}) async-start(), calls=%async_computation.1 | async-start | bytes 8912896 | tf_op jit(solution)/shard_map/reduce_scatter | solution.py:216
  10.1 8.3 copy-start.8
  25.5 7.4 copy-start.14
  44.0 7.3 copy-start.13
  54.8 5.0 copy-start
  62.6 3.0 collective-permute-start
  68.1 7.4 copy-start.14
  86.6 7.3 copy-start.13
  97.4 5.0 copy-start
  105.2 4.0 collective-permute-start
  111.7 7.4 copy-start.14
  130.2 7.3 copy-start.13
  141.0 5.0 copy-start
  148.8 8.3 collective-permute-start
  159.6 7.4 copy-start.14
  178.1 7.3 copy-start.13
  188.9 5.0 copy-start
  196.7 10.7 collective-permute-start
  210.7 47.0 %collective-permute-start = (bf16[60,4096]{1,0:T(8,128)(2,1)}, bf16[60,4096]{1,0:T(8,128)(2,1)S(1)}, u32[]{:S(2)}, u32[]{:S(2)}) collective-permute-start(bf16[60,4096]{1,0:T(8,128)(2,1)} %get-tuple-element.1957), channel_id=1, source_target_pairs={{0,16},{16,32},{32,48},{48,64},{64,80},{80,96},{96,112},{112,128},... | collective-permute-start | bytes 1474568 | tf_op jit(solution)/shard_map/while/body/eval_jaxpr/ppermute | solution.py:20
  261.0 10.7 collective-permute-start
  275.0 47.0 %collective-permute-start = (bf16[60,4096]{1,0:T(8,128)(2,1)}, bf16[60,4096]{1,0:T(8,128)(2,1)S(1)}, u32[]{:S(2)}, u32[]{:S(2)}) collective-permute-start(bf16[60,4096]{1,0:T(8,128)(2,1)} %get-tuple-element.1957), channel_id=1, source_target_pairs={{0,16},{16,32},{32,48},{48,64},{64,80},{80,96},{96,112},{112,128},... | collective-permute-start | bytes 1474568 | tf_op jit(solution)/shard_map/while/body/eval_jaxpr/ppermute | solution.py:20
  325.2 10.7 collective-permute-start
  339.2 33.2 %collective-permute-start = (bf16[60,4096]{1,0:T(8,128)(2,1)}, bf16[60,4096]{1,0:T(8,128)(2,1)S(1)}, u32[]{:S(2)}, u32[]{:S(2)}) collective-permute-start(bf16[60,4096]{1,0:T(8,128)(2,1)} %get-tuple-element.1957), channel_id=1, source_target_pairs={{0,16},{16,32},{32,48},{48,64},{64,80},{80,96},{96,112},{112,128},... | collective-permute-start | bytes 1474568 | tf_op jit(solution)/shard_map/while/body/eval_jaxpr/ppermute | solution.py:20
  375.7 10.7 collective-permute-start
  389.7 44.6 %collective-permute-start = (bf16[60,4096]{1,0:T(8,128)(2,1)}, bf16[60,4096]{1,0:T(8,128)(2,1)S(1)}, u32[]{:S(2)}, u32[]{:S(2)}) collective-permute-start(bf16[60,4096]{1,0:T(8,128)(2,1)} %get-tuple-element.1957), channel_id=1, source_target_pairs={{0,16},{16,32},{32,48},{48,64},{64,80},{80,96},{96,112},{112,128},... | collective-permute-start | bytes 1474568 | tf_op jit(solution)/shard_map/while/body/eval_jaxpr/ppermute | solution.py:20
  437.6 10.7 collective-permute-start
  451.6 33.2 %collective-permute-start = (bf16[60,4096]{1,0:T(8,128)(2,1)}, bf16[60,4096]{1,0:T(8,128)(2,1)S(1)}, u32[]{:S(2)}, u32[]{:S(2)}) collective-permute-start(bf16[60,4096]{1,0:T(8,128)(2,1)} %get-tuple-element.1957), channel_id=1, source_target_pairs={{0,16},{16,32},{32,48},{48,64},{64,80},{80,96},{96,112},{112,128},... | collective-permute-start | bytes 1474568 | tf_op jit(solution)/shard_map/while/body/eval_jaxpr/ppermute | solution.py:20
  488.1 10.7 collective-permute-start
  502.1 44.6 %collective-permute-start = (bf16[60,4096]{1,0:T(8,128)(2,1)}, bf16[60,4096]{1,0:T(8,128)(2,1)S(1)}, u32[]{:S(2)}, u32[]{:S(2)}) collective-permute-start(bf16[60,4096]{1,0:T(8,128)(2,1)} %get-tuple-element.1957), channel_id=1, source_target_pairs={{0,16},{16,32},{32,48},{48,64},{64,80},{80,96},{96,112},{112,128},... | collective-permute-start | bytes 1474568 | tf_op jit(solution)/shard_map/while/body/eval_jaxpr/ppermute | solution.py:20
  550.0 10.7 collective-permute-start
  564.0 33.3 %collective-permute-start = (bf16[60,4096]{1,0:T(8,128)(2,1)}, bf16[60,4096]{1,0:T(8,128)(2,1)S(1)}, u32[]{:S(2)}, u32[]{:S(2)}) collective-permute-start(bf16[60,4096]{1,0:T(8,128)(2,1)} %get-tuple-element.1957), channel_id=1, source_target_pairs={{0,16},{16,32},{32,48},{48,64},{64,80},{80,96},{96,112},{112,128},... | collective-permute-start | bytes 1474568 | tf_op jit(solution)/shard_map/while/body/eval_jaxpr/ppermute | solution.py:20
  600.6 11.9 collective-permute-start
  615.8 48.2 %collective-permute-start = (bf16[60,4096]{1,0:T(8,128)(2,1)}, bf16[60,4096]{1,0:T(8,128)(2,1)S(1)}, u32[]{:S(2)}, u32[]{:S(2)}) collective-permute-start(bf16[60,4096]{1,0:T(8,128)(2,1)} %get-tuple-element.1957), channel_id=1, source_target_pairs={{0,16},{16,32},{32,48},{48,64},{64,80},{80,96},{96,112},{112,128},... | collective-permute-start | bytes 1474568 | tf_op jit(solution)/shard_map/while/body/eval_jaxpr/ppermute | solution.py:20
  668.2 11.8 collective-permute-start.1
  681.5 32.7 %collective-permute-start.1 = (bf16[60,4096]{1,0:T(8,128)(2,1)}, bf16[60,4096]{1,0:T(8,128)(2,1)S(1)}, u32[]{:S(2)}, u32[]{:S(2)}) collective-permute-start(bf16[60,4096]{1,0:T(8,128)(2,1)} %get-tuple-element.1980), channel_id=1, source_target_pairs={{16,0},{32,16},{48,32},{64,48},{80,64},{96,80},{112,96},{128,112},... | collective-permute-start | bytes 1474568 | tf_op jit(solution)/shard_map/while/body/eval_jaxpr/ppermute | solution.py:20
  715.8 11.8 collective-permute-start.1
  729.1 44.1 %collective-permute-start.1 = (bf16[60,4096]{1,0:T(8,128)(2,1)}, bf16[60,4096]{1,0:T(8,128)(2,1)S(1)}, u32[]{:S(2)}, u32[]{:S(2)}) collective-permute-start(bf16[60,4096]{1,0:T(8,128)(2,1)} %get-tuple-element.1980), channel_id=1, source_target_pairs={{16,0},{32,16},{48,32},{64,48},{80,64},{96,80},{112,96},{128,112},... | collective-permute-start | bytes 1474568 | tf_op jit(solution)/shard_map/while/body/eval_jaxpr/ppermute | solution.py:20
  774.8 11.8 collective-permute-start.1
  788.1 32.7 %collective-permute-start.1 = (bf16[60,4096]{1,0:T(8,128)(2,1)}, bf16[60,4096]{1,0:T(8,128)(2,1)S(1)}, u32[]{:S(2)}, u32[]{:S(2)}) collective-permute-start(bf16[60,4096]{1,0:T(8,128)(2,1)} %get-tuple-element.1980), channel_id=1, source_target_pairs={{16,0},{32,16},{48,32},{64,48},{80,64},{96,80},{112,96},{128,112},... | collective-permute-start | bytes 1474568 | tf_op jit(solution)/shard_map/while/body/eval_jaxpr/ppermute | solution.py:20
  822.4 11.8 collective-permute-start.1
  835.7 44.1 %collective-permute-start.1 = (bf16[60,4096]{1,0:T(8,128)(2,1)}, bf16[60,4096]{1,0:T(8,128)(2,1)S(1)}, u32[]{:S(2)}, u32[]{:S(2)}) collective-permute-start(bf16[60,4096]{1,0:T(8,128)(2,1)} %get-tuple-element.1980), channel_id=1, source_target_pairs={{16,0},{32,16},{48,32},{64,48},{80,64},{96,80},{112,96},{128,112},... | collective-permute-start | bytes 1474568 | tf_op jit(solution)/shard_map/while/body/eval_jaxpr/ppermute | solution.py:20
  881.4 11.9 collective-permute-start.1
  894.9 32.5 %collective-permute-start.1 = (bf16[60,4096]{1,0:T(8,128)(2,1)}, bf16[60,4096]{1,0:T(8,128)(2,1)S(1)}, u32[]{:S(2)}, u32[]{:S(2)}) collective-permute-start(bf16[60,4096]{1,0:T(8,128)(2,1)} %get-tuple-element.1980), channel_id=1, source_target_pairs={{16,0},{32,16},{48,32},{64,48},{80,64},{96,80},{112,96},{128,112},... | collective-permute-start | bytes 1474568 | tf_op jit(solution)/shard_map/while/body/eval_jaxpr/ppermute | solution.py:20
  929.0 11.9 collective-permute-start.1
  942.5 43.9 %collective-permute-start.1 = (bf16[60,4096]{1,0:T(8,128)(2,1)}, bf16[60,4096]{1,0:T(8,128)(2,1)S(1)}, u32[]{:S(2)}, u32[]{:S(2)}) collective-permute-start(bf16[60,4096]{1,0:T(8,128)(2,1)} %get-tuple-element.1980), channel_id=1, source_target_pairs={{16,0},{32,16},{48,32},{64,48},{80,64},{96,80},{112,96},{128,112},... | collective-permute-start | bytes 1474568 | tf_op jit(solution)/shard_map/while/body/eval_jaxpr/ppermute | solution.py:20
  988.0 11.9 collective-permute-start.1
  1001.5 32.5 %collective-permute-start.1 = (bf16[60,4096]{1,0:T(8,128)(2,1)}, bf16[60,4096]{1,0:T(8,128)(2,1)S(1)}, u32[]{:S(2)}, u32[]{:S(2)}) collective-permute-start(bf16[60,4096]{1,0:T(8,128)(2,1)} %get-tuple-element.1980), channel_id=1, source_target_pairs={{16,0},{32,16},{48,32},{64,48},{80,64},{96,80},{112,96},{128,112},... | collective-permute-start | bytes 1474568 | tf_op jit(solution)/shard_map/while/body/eval_jaxpr/ppermute | solution.py:20
  1035.6 647.6 %collective-permute-start.1 = (bf16[60,4096]{1,0:T(8,128)(2,1)}, bf16[60,4096]{1,0:T(8,128)(2,1)S(1)}, u32[]{:S(2)}, u32[]{:S(2)}) collective-permute-start(bf16[60,4096]{1,0:T(8,128)(2,1)} %get-tuple-element.1980), channel_id=1, source_target_pairs={{16,0},{32,16},{48,32},{64,48},{80,64},{96,80},{112,96},{128,112},... | collective-permute-start | bytes 1474568 | tf_op jit(solution)/shard_map/while/body/eval_jaxpr/ppermute | solution.py:20
  1701.3 17.0 slice-start
  1703.0 10.5 copy-start.4
  1703.0 15.3 slice-start.1
  1727.7 12.1 collective-permute-start.1
  1757.9 17.0 slice-start
  1759.6 10.5 copy-start.4
  1759.6 15.3 slice-start.1
  1784.3 11.8 collective-permute-start.1
  1814.3 17.0 slice-start
  1816.0 10.5 copy-start.4
  1816.0 15.3 slice-start.1
  1840.7 11.9 collective-permute-start.1
  1870.7 17.0 slice-start
  1872.4 10.5 copy-start.4
  1872.4 15.3 slice-start.1
  1897.1 4.0 collective-permute-start.1
  (57 other events, 127.4 us)
Sparse Core Ops, SparseCore 0:
  1908.4 86.1 reduce-scatter.1
where the time goes:
time: 2010 us; the launch traced here: 2000 us
  waiting for transfers between devices  1090 us (54%)
  starting transfers between devices  425 us (21%)
  other arithmetic  171 us (9%)
  local copies, waits for them, and re-layouts  154 us (8%)
  matrix products  95 us (5%)
  blocking collectives  35.6 us (2%)
    ppermute x38, waiting for transfers between devices, from_behind(): return lax.ppermute(block, axis, route)  1040 us
    ppermute x38, starting transfers between devices, from_behind(): return lax.ppermute(block, axis, route)  425 us
    reduce_scatter x1, waiting for transfers between devices, local(): lax.psum_scatter(local_grads.astype(jnp.bfloat16), 'dp', scatter_dimensio...  48.1 us
    sub x4, other arithmetic, backward_piece(): d_scores = probs * (d_probs - jnp.sum(probs * d_probs, -1, keepdims=True))  42.1 us
    dynamic_update_slice x16, local copies, waits for them, and re-layouts, masked_write(): return lax.dynamic_update_slice_in_dim(buffer, fresh, start, 0)  42 us
  transfers between devices with their start and end apart: 39, of which 39 were waited for; matrix products, arithmetic and copies ran while one was open for 0% of the time, Pallas kernels for 0%

commit v1 on v0

v1 whole, which is shorter than its diff:
```python
import functools
import math

import jax
import jax.numpy as jnp
from jax import lax
from jax.experimental import pallas as pl
from jax.experimental.pallas import tpu as pltpu
from jax.sharding import PartitionSpec as P

HEADS = 32
KV_HEADS = 4
GROUP = 8
HEAD_DIM = 128
SEGS = 4
BLK = 16
EPSILON = 1e-06

T = 32
WINDOW = 128
PAD = WINDOW - T
CHUNK = GROUP * HEAD_DIM
MESH = pl.DeviceIdType.MESH
F32 = jnp.float32
BF16 = jnp.bfloat16
EXP_SCALE = HEAD_DIM**-0.5 * math.log2(math.e)
SCALE = HEAD_DIM**-0.5


def to_rows(block):
    return jnp.concatenate(
        [block[:, HEAD_DIM * g : HEAD_DIM * (g + 1)] for g in range(GROUP)], axis=0
    )


def to_lanes(block):
    return jnp.concatenate([block[T * g : T * (g + 1)] for g in range(GROUP)], axis=1)


def fold_lanes(block):
    total = block[:, :128]
    for g in range(1, block.shape[1] // 128):
        total = total + block[:, 128 * g : 128 * (g + 1)]
    return total


def dot_t(a, b):
    return lax.dot_general(a, b, (((1,), (1,)), ((), ())), preferred_element_type=F32)


def t_dot(a, b):
    return lax.dot_general(a, b, (((0,), (0,)), ((), ())), preferred_element_type=F32)


def dot(a, b):
    return jnp.dot(a, b, preferred_element_type=F32)


def kernel(
    n_sec,
    n_dp,
    tok,
    ups,
    gain,
    w,
    bias,
    fac,
    out_w,
    out_g,
    xb,
    hb,
    gb,
    xo,
    go,
    wb,
    kvb,
    dacc,
    pb,
    dqb,
    rb,
    gf,
    gsum,
    gs,
    hg,
    dg,
    gg,
    w_sem,
    in_sem,
    f_send,
    f_recv,
    g_send,
    g_recv,
    h_send,
    h_recv,
    d_send,
    d_recv,
    s_send,
    s_recv,
):
    sec = lax.axis_index("section")
    me = lax.axis_index("dp")
    seq_len = xb.shape[1]
    pieces = seq_len // T
    width = KV_HEADS * CHUNK
    kv_width = KV_HEADS * HEAD_DIM
    block = width // n_dp
    first = sec == 0
    last = sec == n_sec - 1

    w_copies = [
        pltpu.make_async_copy(w.at[0, pl.ds(k * CHUNK, CHUNK)], wb.at[k], w_sem.at[k])
        for k in range(KV_HEADS)
    ]
    tok_copies = [
        pltpu.make_async_copy(tok.at[0, :, pl.ds(k * CHUNK, CHUNK)], xb.at[k], in_sem.at[k])
        for k in range(KV_HEADS)
    ]
    ups_copies = [
        pltpu.make_async_copy(ups.at[0, :, pl.ds(k * CHUNK, CHUNK)], xo.at[k], in_sem.at[k])
        for k in range(KV_HEADS)
    ]

    @pl.when(first)
    def _():
        for copy in tok_copies:
            copy.start()

    for copy in w_copies:
        copy.start()

    @pl.when(last)
    def _():
        for copy in ups_copies:
            copy.start()

    barrier = pltpu.get_barrier_semaphore()

    for neighbour in ((sec + 1) % n_sec, (sec + n_sec - 1) % n_sec):
        pl.semaphore_signal(
            barrier, inc=1, device_id={"section": neighbour}, device_id_type=MESH
        )
    for j in range(1, n_dp):
        pl.semaphore_signal(
            barrier, inc=1, device_id={"dp": (me + j) % n_dp}, device_id_type=MESH
        )

    kvb[pl.ds(0, PAD), :] = jnp.zeros((PAD, 2 * kv_width), BF16)
    dacc[...] = jnp.zeros_like(dacc)
    gsum[...] = jnp.zeros_like(gsum)
    for k in range(KV_HEADS):
        gf[k] = jnp.broadcast_to(
            gain[:, pl.ds(k * CHUNK, CHUNK)].astype(F32), (8, CHUNK)
        )

    @pl.when(last)
    def _():
        for copy in ups_copies:
            copy.wait()

        def scale_piece(p, carry):
            rows = pl.ds(pl.multiple_of(p * T, T), T)
            factor = fac[rows, :][:, :1]
            for k in range(KV_HEADS):
                gb[k, rows, :] = (xo[k, rows, :].astype(F32) * factor).astype(BF16)
            return carry

        lax.fori_loop(0, pieces, scale_piece, 0)

    for copy in w_copies:
        copy.wait()

    @pl.when(first)
    def _():
        for copy in tok_copies:
            copy.wait()

    pl.semaphore_wait(barrier, n_dp + 1)

    def forward(p, carry):
        start = pl.multiple_of(p * T, T)
        rows = pl.ds(start, T)
        acc = jnp.zeros((T, 2 * kv_width), F32)
        squares = jnp.zeros((T, 128), F32)
        for k in range(KV_HEADS):
            arrival = pltpu.make_async_remote_copy(
                src_ref=xb.at[k, rows],
                dst_ref=xb.at[k, rows],
                send_sem=f_send,
                recv_sem=f_recv.at[p, k],
                device_id={"section": sec},
                device_id_type=MESH,
            )

            @pl.when(sec > 0)
            def _():
                arrival.wait_recv()

            values = xb[k, rows, :].astype(F32)
            squares = squares + fold_lanes(values * values)
            acc = acc + dot((values * gf[k, 0:1, :]).astype(BF16), wb[k])
        inverse = lax.rsqrt(jnp.sum(squares, -1, keepdims=True) / width + EPSILON)
        rb[rows, :] = jnp.broadcast_to(inverse, (T, 128))
        kvb[pl.ds(pl.multiple_of(start + PAD, T), T), :] = (acc * inverse).astype(BF16)
        window = pl.ds(start, WINDOW)
        bias_rows = jnp.concatenate([bias[p]] * GROUP, axis=0)
        for k in range(KV_HEADS):
            values = xb[k, rows, :].astype(F32)
            hidden = (values * inverse * gf[k, 0:1, :]).astype(BF16)
            hb[k, rows, :] = hidden
            keys = kvb[window, pl.ds(k * HEAD_DIM, HEAD_DIM)]
            vals = kvb[window, pl.ds(kv_width + k * HEAD_DIM, HEAD_DIM)]
            scores = dot_t(to_rows(hidden), keys)
            raw = jnp.exp2(scores * EXP_SCALE + bias_rows)
            share = 1.0 / jnp.sum(raw, -1, keepdims=True)
            mixed = dot(raw.astype(BF16), vals) * share
            xo_rows = (values + to_lanes(mixed)).astype(BF16)

            @pl.when(sec < n_sec - 1)
            def _():
                xo[k, rows, :] = xo_rows
                pltpu.make_async_remote_copy(
                    src_ref=xo.at[k, rows],
                    dst_ref=xb.at[k, rows],
                    send_sem=f_send,
                    recv_sem=f_recv.at[p, k],
                    device_id={"section": sec + 1},
                    device_id_type=MESH,
                ).start()

            pb[p, k] = raw * share
        return carry

    lax.fori_loop(0, pieces, forward, 0)

    def to_peer(j, src, dst, send_sem, recv_sem):
        return pltpu.make_async_remote_copy(
            src_ref=src,
            dst_ref=dst,
            send_sem=send_sem,
            recv_sem=recv_sem,
            device_id={"dp": (me + j) % n_dp},
            device_id_type=MESH,
        )

    def block_of(ref, j):
        column = ((me + j) % n_dp) * block
        return ref.at[
            column // CHUNK, :, pl.ds(pl.multiple_of(column % CHUNK, block), block)
        ]

    own_block = pltpu.make_async_copy(block_of(hb, 0), hg.at[0], in_sem.at[0])
    own_block.start()
    for j in range(1, n_dp):
        to_peer(j, block_of(hb, j), hg.at[j], h_send, h_recv).start()

    def backward(step, carry):
        p = pieces - 1 - step
        start = pl.multiple_of(p * T, T)
        rows = pl.ds(start, T)
        window = pl.ds(start, WINDOW)
        own = pl.ds(pl.multiple_of(start + PAD, T), T)
        inner = jnp.zeros((T, 128), F32)
        for k in range(KV_HEADS):
            arrival = pltpu.make_async_remote_copy(
                src_ref=gb.at[k, rows],
                dst_ref=gb.at[k, rows],
                send_sem=g_send,
                recv_sem=g_recv.at[p, k],
                device_id={"section": sec},
                device_id_type=MESH,
            )

            @pl.when(sec < n_sec - 1)
            def _():
                arrival.wait_recv()

            grads = to_rows(gb[k, rows, :])
            hidden = hb[k, rows, :]
            query = to_rows(hidden)
            keys = kvb[window, pl.ds(k * HEAD_DIM, HEAD_DIM)]
            vals = kvb[window, pl.ds(kv_width + k * HEAD_DIM, HEAD_DIM)]
            probs = pb[p, k]
            product = probs * dot_t(grads, vals)
            total = jnp.sum(product, -1, keepdims=True)
            d_low = ((product - probs * total) * SCALE).astype(BF16)
            d_query = to_lanes(dot(d_low, keys))
            dqb[k] = d_query
            inner = inner + fold_lanes(d_query * hidden.astype(F32))
            dacc[k, window, :] += t_dot(d_low, query)
            dacc[KV_HEADS + k, window, :] += t_dot(probs.astype(BF16), grads)
        d_kv = jnp.concatenate([dacc[i, own, :] for i in range(2 * KV_HEADS)], axis=1).astype(
            BF16
        )
        dg[p, 0] = d_kv
        inner = inner + fold_lanes(d_kv.astype(F32) * kvb[own, :].astype(F32))
        mean = jnp.sum(inner, -1, keepdims=True) / width
        inverse = rb[rows, :][:, :1]
        for k in range(KV_HEADS):
            d_hidden = dqb[k] + dot_t(d_kv, wb[k])
            normed = xb[k, rows, :].astype(F32) * inverse
            moment = d_hidden * normed
            gsum[k] += moment[0:8] + moment[8:16] + moment[16:24] + moment[24:32]

            @pl.when(sec > 0)
            def _():
                d_inputs = inverse * (d_hidden * gf[k, 0:1, :] - normed * mean)
                go[k, rows, :] = (gb[k, rows, :].astype(F32) + d_inputs).astype(BF16)
                pltpu.make_async_remote_copy(
                    src_ref=go.at[k, rows],
                    dst_ref=gb.at[k, rows],
                    send_sem=g_send,
                    recv_sem=g_recv.at[p, k],
                    device_id={"section": sec - 1},
                    device_id_type=MESH,
                ).start()

        for j in range(1, n_dp):
            to_peer(j, dg.at[p, 0], dg.at[p, j], d_send, d_recv.at[p]).start()
        return carry

    lax.fori_loop(0, pieces, backward, 0)

    for k in range(KV_HEADS):
        row = jnp.sum(gsum[k], 0, keepdims=True).astype(BF16).astype(F32)
        gs[k] = jnp.broadcast_to(row, (8, CHUNK))
    own_gain = pltpu.make_async_copy(block_of(gs, 0), gg.at[0], in_sem.at[1])
    own_gain.start()
    for j in range(1, n_dp):
        to_peer(j, block_of(gs, j), gg.at[j], s_send, s_recv).start()

    def wait_for(ref, sem):
        pltpu.make_async_copy(ref, ref, sem).wait()

    others = pl.ds(1, n_dp - 1)
    own_block.wait()
    wait_for(hg.at[others], h_recv)

    def multiply(step, carry):
        p = pieces - 1 - step
        rows = pl.ds(pl.multiple_of(p * T, T), T)
        wait_for(dg.at[p, others], d_recv.at[p])
        hidden = hg[:, rows, :].reshape(n_dp * T, block)
        d_kv = dg[p].reshape(n_dp * T, 2 * kv_width)
        product = t_dot(hidden, d_kv)

        @pl.when(step == 0)
        def _():
            out_w[...] = product

        @pl.when(step > 0)
        def _():
            out_w[...] += product

        return carry

    lax.fori_loop(0, pieces, multiply, 0)
    own_gain.wait()
    wait_for(gg.at[others], s_recv)
    gain_total = gg[0]
    for j in range(1, n_dp):
        gain_total = gain_total + gg[j]
    out_g[...] = gain_total[0:1]

    wait_for(hg.at[others], h_send)
    wait_for(dg.at[:, others], d_send)
    wait_for(gg.at[others], s_send)

    @pl.when(sec < n_sec - 1)
    def _():
        wait_for(xo, f_send)

    @pl.when(sec > 0)
    def _():
        wait_for(go, g_send)


def attention_bias(doc_lengths, block_mask, seq_len):
    positions = jnp.arange(seq_len, dtype=jnp.int32)
    doc_ends = jnp.cumsum(doc_lengths)
    doc_ids = jnp.sum((positions[:, None] >= doc_ends[None, :]).astype(jnp.int32), 1)
    blocks = positions // BLK
    opened = jnp.repeat(jnp.repeat(block_mask == 1, BLK, 0), BLK, 1)
    allowed = (
        (positions[None, :] <= positions[:, None])
        & (doc_ids[:, None] == doc_ids[None, :])
        & (opened | (blocks[:, None] == blocks[None, :]))
    )
    full = jnp.pad(jnp.where(allowed, 0.0, -1e30), ((0, 0), (PAD, 0)), constant_values=-1e30)
    return jnp.stack(
        [full[s : s + T, s : s + WINDOW] for s in range(0, seq_len, T)]
    ).astype(F32)


def row_factor(seg_lengths, seq_len):
    positions = jnp.arange(seq_len, dtype=jnp.int32)
    seg_ends = jnp.cumsum(seg_lengths)
    seg_ids = jnp.sum((positions[:, None] >= seg_ends[None, :]).astype(jnp.int32), 1)
    sizes = jnp.sum(
        jnp.where(seg_ids[:, None] == jnp.arange(SEGS)[None, :], seg_lengths[None, :], 0), 1
    )
    factor = seq_len / (SEGS * sizes.astype(F32))
    return jnp.broadcast_to(factor[:, None], (seq_len, 128))


def local(n_sec, n_dp, tokens, upstream, gains, w_kv, doc_lengths, seg_lengths, block_mask):
    seq_len, width = tokens.shape[1:]
    pieces = seq_len // T
    kv2 = w_kv.shape[2]
    block = width // n_dp
    bias = attention_bias(doc_lengths[0], block_mask[0], seq_len)
    factor = row_factor(seg_lengths[0], seq_len)
    any_spec = pl.BlockSpec(memory_space=pl.ANY)
    vmem = pl.BlockSpec(memory_space=pltpu.VMEM)
    features = (KV_HEADS, seq_len, CHUNK)
    dma = pltpu.SemaphoreType.DMA
    grad_weight, grad_gain = pl.pallas_call(
        functools.partial(kernel, n_sec, n_dp),
        out_shape=(
            jax.ShapeDtypeStruct((block, kv2), F32),
            jax.ShapeDtypeStruct((1, block), F32),
        ),
        in_specs=[any_spec, any_spec, vmem, any_spec, vmem, vmem],
        out_specs=(vmem, vmem),
        scratch_shapes=[
            pltpu.VMEM(features, BF16),
            pltpu.VMEM(features, BF16),
            pltpu.VMEM(features, BF16),
            pltpu.VMEM(features, BF16),
            pltpu.VMEM(features, BF16),
            pltpu.VMEM((KV_HEADS, CHUNK, kv2), BF16),
            pltpu.VMEM((PAD + seq_len, kv2), BF16),
            pltpu.VMEM((2 * KV_HEADS, PAD + seq_len, HEAD_DIM), F32),
            pltpu.VMEM((pieces, KV_HEADS, GROUP * T, WINDOW), F32),
            pltpu.VMEM((KV_HEADS, T, CHUNK), F32),
            pltpu.VMEM((seq_len, 128), F32),
            pltpu.VMEM((KV_HEADS, 8, CHUNK), F32),
            pltpu.VMEM((KV_HEADS, 8, CHUNK), F32),
            pltpu.VMEM((KV_HEADS, 8, CHUNK), F32),
            pltpu.VMEM((n_dp, seq_len, block), BF16),
            pltpu.VMEM((pieces, n_dp, T, kv2), BF16),
            pltpu.VMEM((n_dp, 8, block), F32),
            dma((KV_HEADS,)),
            dma((KV_HEADS,)),
            dma,
            dma((pieces, KV_HEADS)),
            dma,
            dma((pieces, KV_HEADS)),
            dma,
            dma,
            dma,
            dma((pieces,)),
            dma,
            dma,
        ],
        compiler_params=pltpu.CompilerParams(
            collective_id=0, has_side_effects=True, vmem_limit_bytes=52 * 1024 * 1024
        ),
        cost_estimate=pl.CostEstimate(
            flops=7 * 10**9, bytes_accessed=12 * 2**20, transcendentals=10**6
        ),
        name="relay",
    )(tokens, upstream, gains, w_kv, bias, factor)
    return grad_weight[None], grad_gain


def solution(mesh):
    placed = (
        P("dp", None, None),
        P("dp", None, None),
        P("section", None),
        P("section", None, None),
        P("dp", None),
        P("dp", None),
        P("dp", None, None),
    )
    return jax.shard_map(
        functools.partial(local, mesh.shape["section"], mesh.shape["dp"]),
        mesh=mesh,
        in_specs=placed,
        out_specs=(P("section", "dp", None), P("section", "dp")),
        check_vma=False,
    )
```

time: 2010 us -> 258 us (0.13)
  waiting for transfers between devices: 1090 us -> 0 us
  starting transfers between devices: 425 us -> 0 us
  Pallas kernels: 0 us -> 246 us
  other arithmetic: 171 us -> 3.41 us
  local copies, waits for them, and re-layouts: 154 us -> 3.17 us
  matrix products: 95 us -> 0 us
  blocking collectives: 35.6 us -> 0 us
    ppermute x38 -> x0, waiting for transfers between devices: 1040 us -> none  [from_behind(): return lax.ppermute(block, axis, route)]
    ppermute x38 -> x0, starting transfers between devices: 425 us -> none  [from_behind(): return lax.ppermute(block, axis, route)]
    pallas_call x0 -> x1, Pallas kernels: none -> 246 us  [local(): pl.pallas_call(functools.partial(kernel, n_sec, n_dp), out_shape=(jax.Sha...]
    dot_general x45 -> x0, matrix products: 95 us -> none  [the longest x4 19.8 us: forward_piece(): jnp.dot(hidden_win, weight, preferred_element_type=jnp.float32)]
    convert_element_type x50 -> x0, other arithmetic: 48.7 us -> none  [the longest x38 36.9 us: local(): (jnp.arange(blocks)[:, None] == key_blocks[None, :]).astype(jnp.float32)]
    reduce_scatter x1 -> x0, waiting for transfers between devices: 48.1 us -> none  [local(): lax.psum_scatter(local_grads.astype(jnp.bfloat16), 'dp', scatter_dimensio...]
    sub x5 -> x0, other arithmetic: 43.4 us -> none  [the longest x4 42.1 us: backward_piece(): d_scores = probs * (d_probs - jnp.sum(probs * d_probs, -1, keepdims=True))]
    dynamic_update_slice x16 -> x0, local copies, waits for them, and re-layouts: 42 us -> none  [masked_write(): return lax.dynamic_update_slice_in_dim(buffer, fresh, start, 0)]
  transfers between devices with their start and end apart: 39 -> 0, of which waited for: 39 -> 0; matrix products, arithmetic and copies ran while one was open for 0% -> 0% of each run, Pallas kernels for 0% -> 0%
where the time goes in v1:
time: 258 us; the launch traced here: 254 us
  Pallas kernels  246 us (95%)
  other arithmetic  3.41 us (1%)
  local copies, waits for them, and re-layouts  3.17 us (1%)
    pallas_call x1, Pallas kernels, local(): pl.pallas_call(functools.partial(kernel, n_sec, n_dp), out_shape=(jax.Sha...  246 us

profile of v1, /device:TPU:2, one launch (start us, length us, event | category | flops | bytes accessed | tf_op | source)
XLA Modules:
  0.0 253.8 jit_solution(11152315526115495140)
XLA Ops:
  0.6 0.8 reduce-window.16
  1.5 0.1 convert_reduce_fusion.1
  1.5 0.8 reduce-window.17
  2.4 0.1 convert_reduce_fusion
  2.5 0.7 select_reduce_fusion
  3.2 0.7 broadcast_compare_fusion
  3.9 0.1 copy.13
  4.0 0.1 broadcast_in_dim.30
  4.1 0.1 reshape.96
  4.3 0.1 copy.12
  4.4 0.1 broadcast_in_dim.56.fac
  4.5 0.1 fusion.2
  4.6 0.1 fusion.4
  4.7 0.1 fusion.6
  4.8 0.1 fusion.8
  4.9 0.1 fusion.10
  4.9 0.1 fusion.9.bias
  5.0 0.0 copy-start
  5.0 0.7 copy-done
  5.7 246.5 %relay.1 = (f32[256,1024]{1,0:T(8,128)S(1)}, f32[1,256]{1,0:T(1,128)S(1)}) custom-call(bf16[1,192,4096]{2,1,0:T(8,128)(2,1)} %tok.1, bf16[1,192,4096]{2,1,0:T(8,128)(2,1)} %ups.1, bf16[1,4096]{1,0:T(2,128)(2,1)S(1)} %copy-done, bf16[1,4096,1024]{2,1,0:T(8,128)(2,1)} %w.1, f32[6,32,128]{2,1,0:T(8,128)S(1)} %fusion.9.bias, f32[192,128]{1,0:T(8,128)S(1)} %broadcast_in_dim.56.fac), custom_call_target="tpu_custom_call" | custom-call | flops 7000000000 | bytes 12582912 | tf_op jit(solution)/shard_map/relay/pallas_call | solution.py:416
  252.2 1.0 copy.21
  253.2 0.6 copy.22
  (4 shorter events, 0.0 us)
Async XLA Ops:
  5.0 0.7 copy-start

commit v2 on v1

v2 whole, which is shorter than its diff:
```python
import functools
import math

import jax
import jax.numpy as jnp
from jax import lax
from jax.experimental import pallas as pl
from jax.experimental.pallas import tpu as pltpu
from jax.sharding import PartitionSpec as P

HEADS = 32
KV_HEADS = 4
GROUP = 8
HEAD_DIM = 128
SEGS = 4
BLK = 16
EPSILON = 1e-06

T = 32
WINDOW = 128
PAD = WINDOW - T
CHUNK = GROUP * HEAD_DIM
MESH = pl.DeviceIdType.MESH
F32 = jnp.float32
BF16 = jnp.bfloat16
EXP_SCALE = HEAD_DIM**-0.5 * math.log2(math.e)
SCALE = HEAD_DIM**-0.5


def to_rows(block):
    return jnp.concatenate(
        [block[:, HEAD_DIM * g : HEAD_DIM * (g + 1)] for g in range(GROUP)], axis=0
    )


def to_lanes(block):
    return jnp.concatenate([block[T * g : T * (g + 1)] for g in range(GROUP)], axis=1)


def fold_lanes(block):
    total = block[:, :128]
    for g in range(1, block.shape[1] // 128):
        total = total + block[:, 128 * g : 128 * (g + 1)]
    return total


def dot_t(a, b):
    return lax.dot_general(a, b, (((1,), (1,)), ((), ())), preferred_element_type=F32)


def t_dot(a, b):
    return lax.dot_general(a, b, (((0,), (0,)), ((), ())), preferred_element_type=F32)


def dot(a, b):
    return jnp.dot(a, b, preferred_element_type=F32)


def kernel(
    n_sec,
    n_dp,
    tok,
    ups,
    gain,
    w,
    docs,
    segs,
    table,
    out_w,
    out_g,
    xb,
    hb,
    gb,
    xo,
    go,
    wb,
    wt,
    kvb,
    dacc,
    pb,
    pt,
    dqb,
    rb,
    bias,
    gf,
    gsum,
    gs,
    hg,
    ht,
    do,
    dg,
    wacc,
    eo,
    eg,
    gg,
    w_sem,
    in_sem,
    f_send,
    f_recv,
    g_send,
    g_recv,
    h_send,
    h_recv,
    d_send,
    d_recv,
    e_send,
    e_recv,
    s_send,
    s_recv,
):
    sec = lax.axis_index("section")
    me = lax.axis_index("dp")
    seq_len = xb.shape[1]
    pieces = seq_len // T
    width = KV_HEADS * CHUNK
    kv_width = KV_HEADS * HEAD_DIM
    block = width // n_dp
    grid_y = n_dp // KV_HEADS
    cols = 2 * kv_width // grid_y
    x, y = me // grid_y, me % grid_y
    first = sec == 0
    last = sec == n_sec - 1
    early = sec < (n_sec + 3) // 4

    w_copies = [
        pltpu.make_async_copy(w.at[0, pl.ds(k * CHUNK, CHUNK)], wb.at[k], w_sem.at[k])
        for k in range(KV_HEADS)
    ]
    tok_copies = [
        pltpu.make_async_copy(tok.at[0, :, pl.ds(k * CHUNK, CHUNK)], xb.at[k], in_sem.at[k])
        for k in range(KV_HEADS)
    ]
    ups_copies = [
        pltpu.make_async_copy(ups.at[0, :, pl.ds(k * CHUNK, CHUNK)], xo.at[k], in_sem.at[k])
        for k in range(KV_HEADS)
    ]

    @pl.when(first)
    def _():
        for copy in tok_copies:
            copy.start()

    for copy in w_copies:
        copy.start()

    @pl.when(last)
    def _():
        for copy in ups_copies:
            copy.start()

    barrier = pltpu.get_barrier_semaphore()
    for neighbour in ((sec + 1) % n_sec, (sec + n_sec - 1) % n_sec):
        pl.semaphore_signal(
            barrier, inc=1, device_id={"section": neighbour}, device_id_type=MESH
        )
    for j in range(1, n_dp):
        pl.semaphore_signal(
            barrier, inc=1, device_id={"dp": (me + j) % n_dp}, device_id_type=MESH
        )

    kvb[pl.ds(0, PAD), :] = jnp.zeros((PAD, 2 * kv_width), BF16)
    dacc[...] = jnp.zeros_like(dacc)
    gsum[...] = jnp.zeros_like(gsum)
    for k in range(KV_HEADS):
        gf[k] = jnp.broadcast_to(
            gain[:, pl.ds(k * CHUNK, CHUNK)].astype(F32), (8, CHUNK)
        )

    doc_ends = [docs[0, 0]]
    for d in range(1, docs.shape[1] - 1):
        doc_ends.append(doc_ends[-1] + docs[0, d])

    def doc_of(positions):
        total = jnp.zeros_like(positions)
        for end in doc_ends:
            total = total + jnp.where(positions >= end, 1, 0)
        return total

    row = lax.broadcasted_iota(jnp.int32, (T, WINDOW), 0)
    column = lax.broadcasted_iota(jnp.int32, (T, WINDOW), 1)

    def mask_piece(p, carry):
        queries = row + p * T
        keys = column + (p * T - PAD)
        first_block = p * (T // BLK)
        opened = jnp.zeros((T, WINDOW), jnp.int32)
        for a in range(T // BLK):
            line = jnp.zeros((T, WINDOW), jnp.int32)
            for c in range(WINDOW // BLK):
                key_block = first_block + c - PAD // BLK
                value = table[0, first_block + a, jnp.maximum(key_block, 0)]
                line = jnp.where(column // BLK == c, value, line)
            opened = jnp.where(row // BLK == a, line, opened)
        same = row // BLK + PAD // BLK == column // BLK
        allowed = (
            (keys >= 0)
            & (keys <= queries)
            & (doc_of(keys) == doc_of(queries))
            & (same | (opened == 1))
        )
        bias[p] = jnp.where(allowed, 0.0, -1e30)
        return carry

    lax.fori_loop(0, pieces, mask_piece, 0)

    @pl.when(last)
    def _():
        for copy in ups_copies:
            copy.wait()
        sizes = [segs[0, i] for i in range(SEGS)]

        def scale_piece(p, carry):
            rows = pl.ds(pl.multiple_of(p * T, T), T)
            positions = row + p * T
            count = jnp.zeros((T, WINDOW), jnp.int32) + sizes[0]
            end = sizes[0]
            for i in range(1, SEGS):
                count = jnp.where(positions >= end, sizes[i], count)
                end = end + sizes[i]
            factor = seq_len / (SEGS * count.astype(F32))
            factor = jnp.concatenate([factor] * (CHUNK // WINDOW), axis=1)
            for k in range(KV_HEADS):
                gb[k, rows, :] = (xo[k, rows, :].astype(F32) * factor).astype(BF16)
            return carry

        lax.fori_loop(0, pieces, scale_piece, 0)

    for copy in w_copies:
        copy.wait()

    @pl.when(first)
    def _():
        for copy in tok_copies:
            copy.wait()

    def transpose_w():
        def part(i, carry):
            k, c = i // 4, i % 4
            source = pl.ds(pl.multiple_of(c * 256, 256), 256)
            for n in range(2 * kv_width // 256):
                wt[k, pl.ds(n * 256, 256), source] = wb[k, source, pl.ds(n * 256, 256)].T
            return carry

        lax.fori_loop(0, KV_HEADS * (CHUNK // 256), part, 0)

    @pl.when(jnp.logical_not(early))
    def _():
        transpose_w()

    pl.semaphore_wait(barrier, n_dp + 1)

    def forward(p, carry):
        start = pl.multiple_of(p * T, T)
        rows = pl.ds(start, T)
        acc = jnp.zeros((T, 2 * kv_width), F32)
        squares = jnp.zeros((T, 128), F32)
        for k in range(KV_HEADS):
            arrival = pltpu.make_async_remote_copy(
                src_ref=xb.at[k, rows],
                dst_ref=xb.at[k, rows],
                send_sem=f_send,
                recv_sem=f_recv.at[p, k],
                device_id={"section": sec},
                device_id_type=MESH,
            )

            @pl.when(sec > 0)
            def _():
                arrival.wait_recv()

            values = xb[k, rows, :].astype(F32)
            squares = squares + fold_lanes(values * values)
            acc = acc + dot((values * gf[k, 0:1, :]).astype(BF16), wb[k])
        inverse = lax.rsqrt(jnp.sum(squares, -1, keepdims=True) / width + EPSILON)
        rb[rows, :] = jnp.broadcast_to(inverse, (T, 128))
        kvb[pl.ds(pl.multiple_of(start + PAD, T), T), :] = (acc * inverse).astype(BF16)
        window = pl.ds(start, WINDOW)
        bias_rows = jnp.concatenate([bias[p]] * GROUP, axis=0)
        for k in range(KV_HEADS):
            values = xb[k, rows, :].astype(F32)
            hidden = (values * inverse * gf[k, 0:1, :]).astype(BF16)
            hb[k, rows, :] = hidden
            keys = kvb[window, pl.ds(k * HEAD_DIM, HEAD_DIM)]
            vals = kvb[window, pl.ds(kv_width + k * HEAD_DIM, HEAD_DIM)]
            scores = dot_t(to_rows(hidden), keys)
            raw = jnp.exp2(scores * EXP_SCALE + bias_rows)
            share = 1.0 / jnp.sum(raw, -1, keepdims=True)
            mixed = dot(raw.astype(BF16), vals) * share
            xo[k, rows, :] = (values + to_lanes(mixed)).astype(BF16)
            probs = raw * share
            pb[p, k] = probs
            pt[p, k] = probs.T

        @pl.when(sec < n_sec - 1)
        def _():
            for k in range(KV_HEADS):
                pltpu.make_async_remote_copy(
                    src_ref=xo.at[k, rows],
                    dst_ref=xb.at[k, rows],
                    send_sem=f_send,
                    recv_sem=f_recv.at[p, k],
                    device_id={"section": sec + 1},
                    device_id_type=MESH,
                ).start()

        return carry

    lax.fori_loop(0, pieces, forward, 0)

    def to_peer(dp, src, dst, send_sem, recv_sem):
        return pltpu.make_async_remote_copy(
            src_ref=src,
            dst_ref=dst,
            send_sem=send_sem,
            recv_sem=recv_sem,
            device_id={"dp": dp},
            device_id_type=MESH,
        )

    def wait_for(ref, sem):
        pltpu.make_async_copy(ref, ref, sem).wait()

    peers = []
    for jx in range(KV_HEADS):
        for jy in range(grid_y):
            peer_x, peer_y = (x + jx) % KV_HEADS, (y + jy) % grid_y
            peers.append((jx * grid_y + jy, peer_x * grid_y + peer_y, peer_x, peer_y))
    others = pl.ds(1, n_dp - 1)

    own_hidden = pltpu.make_async_copy(hb.at[x], hg.at[0], in_sem.at[0])
    own_hidden.start()
    for j, dp, peer_x, peer_y in peers[1:]:
        to_peer(dp, hb.at[peer_x], hg.at[j], h_send, h_recv).start()

    def transpose_h():
        own_hidden.wait()
        wait_for(hg.at[others], h_recv)

        def part(p, carry):
            rows = pl.ds(pl.multiple_of(p * T, T), T)
            for c in range(CHUNK // 256):
                hidden = hg[:, rows, pl.ds(c * 256, 256)].reshape(n_dp * T, 256)
                ht[p, pl.ds(c * 256, 256), :] = hidden.T
            return carry

        lax.fori_loop(0, pieces, part, 0)

    @pl.when(early)
    def _():
        transpose_w()
        transpose_h()

    def backward(step, carry):
        p = pieces - 1 - step
        start = pl.multiple_of(p * T, T)
        rows = pl.ds(start, T)
        window = pl.ds(start, WINDOW)
        own = pl.ds(pl.multiple_of(start + PAD, T), T)
        inner = jnp.zeros((T, 128), F32)
        for k in range(KV_HEADS):
            if k % 2 == 0:

                @pl.when(sec < n_sec - 1)
                def _():
                    for i in (k, k + 1):
                        pltpu.make_async_remote_copy(
                            src_ref=gb.at[i, rows],
                            dst_ref=gb.at[i, rows],
                            send_sem=g_send,
                            recv_sem=g_recv.at[p, i],
                            device_id={"section": sec},
                            device_id_type=MESH,
                        ).wait_recv()

            grads = to_rows(gb[k, rows, :])
            hidden = hb[k, rows, :]
            query = to_rows(hidden)
            keys = kvb[window, pl.ds(k * HEAD_DIM, HEAD_DIM)]
            vals = kvb[window, pl.ds(kv_width + k * HEAD_DIM, HEAD_DIM)]
            probs = pb[p, k]
            product = probs * dot_t(grads, vals)
            total = jnp.sum(product, -1, keepdims=True)
            d_low = ((product - probs * total) * SCALE).astype(BF16)
            probs_t = pt[p, k]
            product_t = probs_t * dot_t(vals, grads)
            total_t = jnp.sum(product_t, 0, keepdims=True)
            d_low_t = ((product_t - probs_t * total_t) * SCALE).astype(BF16)
            d_query = to_lanes(dot(d_low, keys))
            dqb[k] = d_query
            inner = inner + fold_lanes(d_query * hidden.astype(F32))
            dacc[k, window, :] += dot(d_low_t, query)
            dacc[KV_HEADS + k, window, :] += dot(probs_t.astype(BF16), grads)
        d_kv = jnp.concatenate([dacc[i, own, :] for i in range(2 * KV_HEADS)], axis=1).astype(
            BF16
        )
        for c in range(grid_y):
            do[p, c] = d_kv[:, c * cols : (c + 1) * cols]
        inner = inner + fold_lanes(d_kv.astype(F32) * kvb[own, :].astype(F32))
        mean = jnp.sum(inner, -1, keepdims=True) / width
        inverse = rb[rows, :][:, :1]

        def send_d_kv():
            dg[p, 0] = do[p, y]
            for j, dp, peer_x, peer_y in peers[1:]:
                to_peer(dp, do.at[p, peer_y], dg.at[p, j], d_send, d_recv.at[p]).start()

        @pl.when(first)
        def _():
            send_d_kv()

        def send_grads(chunks):
            @pl.when(sec > 0)
            def _():
                for k in chunks:
                    pltpu.make_async_remote_copy(
                        src_ref=go.at[k, rows],
                        dst_ref=gb.at[k, rows],
                        send_sem=g_send,
                        recv_sem=g_recv.at[p, k],
                        device_id={"section": sec - 1},
                        device_id_type=MESH,
                    ).start()

        for k in range(KV_HEADS):
            d_hidden = dqb[k] + dot(d_kv, wt[k])
            normed = xb[k, rows, :].astype(F32) * inverse
            moment = d_hidden * normed
            gsum[k] += moment[0:8] + moment[8:16] + moment[16:24] + moment[24:32]
            d_inputs = inverse * (d_hidden * gf[k, 0:1, :] - normed * mean)
            go[k, rows, :] = (gb[k, rows, :].astype(F32) + d_inputs).astype(BF16)
            if k < 2:
                send_grads([k])
            elif k == KV_HEADS - 1:
                send_grads([k - 1, k])

        @pl.when(sec > 0)
        def _():
            send_d_kv()

        return carry

    lax.fori_loop(0, pieces, backward, 0)

    def gain_block(dp):
        column = dp * block
        return gs.at[
            column // CHUNK, :, pl.ds(pl.multiple_of(column % CHUNK, block), block)
        ]

    for k in range(KV_HEADS):
        total = jnp.sum(gsum[k], 0, keepdims=True).astype(BF16).astype(F32)
        gs[k] = jnp.broadcast_to(total, (8, CHUNK))
    own_gain = pltpu.make_async_copy(gain_block(me), gg.at[0], in_sem.at[1])
    own_gain.start()
    for j, dp, peer_x, peer_y in peers[1:]:
        to_peer(dp, gain_block(dp), gg.at[j], s_send, s_recv).start()

    @pl.when(jnp.logical_not(early))
    def _():
        transpose_h()

    def multiply(step, carry):
        p = pieces - 1 - step
        wait_for(dg.at[p, others], d_recv.at[p])
        d_kv = dg[p].reshape(n_dp * T, cols)
        for c in range(CHUNK // 256):
            part = pl.ds(c * 256, 256)
            product = dot(ht[p, part, :], d_kv)
            wacc[part, :] = product + jnp.where(step > 0, wacc[part, :], 0.0)
        return carry

    lax.fori_loop(0, pieces - 1, multiply, 0)
    wait_for(dg.at[0, others], d_recv.at[0])
    d_kv = dg[0].reshape(n_dp * T, cols)
    for jy in list(range(1, grid_y)) + [0]:
        peer_y = (y + jy) % grid_y
        part = pl.ds(pl.multiple_of(peer_y * block, block), block)
        total = wacc[part, :] + dot(ht[0, part, :], d_kv)
        if jy == 0:
            out_w[:, pl.ds(pl.multiple_of(y * cols, cols), cols)] = total
        else:
            eo[jy] = total.astype(BF16)
            to_peer(
                x * grid_y + peer_y, eo.at[jy], eg.at[jy], e_send, e_recv.at[jy]
            ).start()

    own_gain.wait()
    wait_for(gg.at[others], s_recv)
    gain_total = gg[0]
    for j in range(1, n_dp):
        gain_total = gain_total + gg[j]
    out_g[...] = gain_total[0:1]

    for jy in range(1, grid_y):
        wait_for(eg.at[jy], e_recv.at[jy])
        source_y = (y + grid_y - jy) % grid_y
        out_w[:, pl.ds(pl.multiple_of(source_y * cols, cols), cols)] = eg[jy].astype(F32)

    if grid_y > 1:
        wait_for(eo.at[pl.ds(1, grid_y - 1)], e_send)
    wait_for(hg.at[others], h_send)
    wait_for(dg.at[:, others], d_send)
    wait_for(gg.at[others], s_send)

    @pl.when(sec < n_sec - 1)
    def _():
        wait_for(xo, f_send)

    @pl.when(sec > 0)
    def _():
        wait_for(go, g_send)


def local(n_sec, n_dp, tokens, upstream, gains, w_kv, doc_lengths, seg_lengths, block_mask):
    seq_len, width = tokens.shape[1:]
    pieces = seq_len // T
    kv2 = w_kv.shape[2]
    block = width // n_dp
    grid_y = n_dp // KV_HEADS
    cols = kv2 // grid_y
    any_spec = pl.BlockSpec(memory_space=pl.ANY)
    vmem = pl.BlockSpec(memory_space=pltpu.VMEM)
    smem = pl.BlockSpec(memory_space=pltpu.SMEM)
    features = (KV_HEADS, seq_len, CHUNK)
    dma = pltpu.SemaphoreType.DMA
    grad_weight, grad_gain = pl.pallas_call(
        functools.partial(kernel, n_sec, n_dp),
        out_shape=(
            jax.ShapeDtypeStruct((block, kv2), F32),
            jax.ShapeDtypeStruct((1, block), F32),
        ),
        in_specs=[any_spec, any_spec, vmem, any_spec, smem, smem, smem],
        out_specs=(vmem, vmem),
        scratch_shapes=[
            pltpu.VMEM(features, BF16),
            pltpu.VMEM(features, BF16),
            pltpu.VMEM(features, BF16),
            pltpu.VMEM(features, BF16),
            pltpu.VMEM(features, BF16),
            pltpu.VMEM((KV_HEADS, CHUNK, kv2), BF16),
            pltpu.VMEM((KV_HEADS, kv2, CHUNK), BF16),
            pltpu.VMEM((PAD + seq_len, kv2), BF16),
            pltpu.VMEM((2 * KV_HEADS, PAD + seq_len, HEAD_DIM), F32),
            pltpu.VMEM((pieces, KV_HEADS, GROUP * T, WINDOW), F32),
            pltpu.VMEM((pieces, KV_HEADS, WINDOW, GROUP * T), F32),
            pltpu.VMEM((KV_HEADS, T, CHUNK), F32),
            pltpu.VMEM((seq_len, 128), F32),
            pltpu.VMEM((pieces, T, WINDOW), F32),
            pltpu.VMEM((KV_HEADS, 8, CHUNK), F32),
            pltpu.VMEM((KV_HEADS, 8, CHUNK), F32),
            pltpu.VMEM((KV_HEADS, 8, CHUNK), F32),
            pltpu.VMEM((n_dp, seq_len, CHUNK), BF16),
            pltpu.VMEM((pieces, CHUNK, n_dp * T), BF16),
            pltpu.VMEM((pieces, grid_y, T, cols), BF16),
            pltpu.VMEM((pieces, n_dp, T, cols), BF16),
            pltpu.VMEM((CHUNK, cols), F32),
            pltpu.VMEM((grid_y, block, cols), BF16),
            pltpu.VMEM((grid_y, block, cols), BF16),
            pltpu.VMEM((n_dp, 8, block), F32),
            dma((KV_HEADS,)),
            dma((KV_HEADS,)),
            dma,
            dma((pieces, KV_HEADS)),
            dma,
            dma((pieces, KV_HEADS)),
            dma,
            dma,
            dma,
            dma((pieces,)),
            dma,
            dma((grid_y,)),
            dma,
            dma,
        ],
        compiler_params=pltpu.CompilerParams(
            collective_id=0, has_side_effects=True, vmem_limit_bytes=60 * 1024 * 1024
        ),
        cost_estimate=pl.CostEstimate(
            flops=7 * 10**9, bytes_accessed=12 * 2**20, transcendentals=10**6
        ),
        name="relay",
    )(tokens, upstream, gains, w_kv, doc_lengths, seg_lengths, block_mask)
    return grad_weight[None], grad_gain


def solution(mesh):
    placed = (
        P("dp", None, None),
        P("dp", None, None),
        P("section", None),
        P("section", None, None),
        P("dp", None),
        P("dp", None),
        P("dp", None, None),
    )
    return jax.shard_map(
        functools.partial(local, mesh.shape["section"], mesh.shape["dp"]),
        mesh=mesh,
        in_specs=placed,
        out_specs=(P("section", "dp", None), P("section", "dp")),
        check_vma=False,
    )
```

time: 258 us -> 218 us (0.84)
  the two profiles are of different devices: /device:TPU:2 before, /device:TPU:229 now
where the time goes in v2:
time: 218 us
  Pallas kernels  213 us (98%)
  local copies, waits for them, and re-layouts  4.16 us (2%)
    pallas_call x1, Pallas kernels, local(): pl.pallas_call(functools.partial(kernel, n_sec, n_dp), out_shape=(jax.Sha...  213 us

profile of v2, /device:TPU:229, one launch (start us, length us, event | category | flops | bytes accessed | tf_op | source)
XLA Modules:
  0.0 218.1 jit_solution(7465509345614479236)
XLA Ops:
  0.6 1.3 copy.9.table
  1.9 213.3 %relay.1 = (f32[256,1024]{1,0:T(8,128)}, f32[1,256]{1,0:T(1,128)}) custom-call(bf16[1,192,4096]{2,1,0:T(8,128)(2,1)} %tok.1, bf16[1,192,4096]{2,1,0:T(8,128)(2,1)} %ups.1, bf16[1,4096]{1,0:T(2,128)(2,1)} %gain.1, bf16[1,4096,1024]{2,1,0:T(8,128)(2,1)} %w.1, s32[1,4]{1,0:T(1,128)} %docs.1, s32[1,4]{1,0:T(1,128)} %segs.1, s32[1,12,12]{2,1,0:T(8,128)} %copy.9.table), custom_call_target="tpu_custom_call" | custom-call | flops 7000000000 | bytes 12582912 | tf_op jit(solution)/shard_map/relay/pallas_call | solution.py:526
  215.3 0.0 copy-start
  215.3 2.3 %copy.12 = f32[1,256,1024]{2,1,0:T(8,128)} copy(f32[1,256,1024]{2,1,0:T(8,128)} %bitcast.1) | data formatting | bytes 2097152
  217.6 0.0 copy-done
  217.6 0.6 copy.13
Async XLA Ops:
  215.3 2.3 %copy-start = (f32[1,256]{1,0:T(1,128)S(1)}, f32[1,256]{1,0:T(1,128)}, u32[]{:S(2)}) copy-start(f32[1,256]{1,0:T(1,128)} %get-tuple-element.9) | copy-start | bytes 3076

commit v3 on v2

--- a/solution.py
+++ b/solution.py
@@ -16,7 +16,8 @@
 BLK = 16
 EPSILON = 1e-06
 
-T = 32
+T = 16
+SPAN = 2
 WINDOW = 128
 PAD = WINDOW - T
 CHUNK = GROUP * HEAD_DIM
@@ -99,8 +100,12 @@
     f_recv,
     g_send,
     g_recv,
-    h_send,
-    h_recv,
+    hx_send,
+    hx_recv,
+    hy_send,
+    hy_recv,
+    hr_send,
+    hr_recv,
     d_send,
     d_recv,
     e_send,
@@ -118,6 +123,7 @@
     grid_y = n_dp // KV_HEADS
     cols = 2 * kv_width // grid_y
     x, y = me // grid_y, me % grid_y
+    span_rows = SPAN * T
     first = sec == 0
     last = sec == n_sec - 1
     early = sec < (n_sec + 3) // 4
@@ -179,29 +185,22 @@
     row = lax.broadcasted_iota(jnp.int32, (T, WINDOW), 0)
     column = lax.broadcasted_iota(jnp.int32, (T, WINDOW), 1)
 
-    def mask_piece(p, carry):
+    blocks = seq_len // BLK
+    opened = table[0].astype(BF16)
+    block_row = lax.broadcasted_iota(jnp.int32, (blocks, WINDOW), 0)
+    block_column = lax.broadcasted_iota(jnp.int32, (blocks, WINDOW), 1) // BLK
+    for p in range(pieces):
         queries = row + p * T
         keys = column + (p * T - PAD)
-        first_block = p * (T // BLK)
-        opened = jnp.zeros((T, WINDOW), jnp.int32)
-        for a in range(T // BLK):
-            line = jnp.zeros((T, WINDOW), jnp.int32)
-            for c in range(WINDOW // BLK):
-                key_block = first_block + c - PAD // BLK
-                value = table[0, first_block + a, jnp.maximum(key_block, 0)]
-                line = jnp.where(column // BLK == c, value, line)
-            opened = jnp.where(row // BLK == a, line, opened)
-        same = row // BLK + PAD // BLK == column // BLK
+        spread = (block_row == block_column + (p * T - PAD) // BLK).astype(BF16)
+        line = dot(opened, spread)[p : p + 1]
         allowed = (
             (keys >= 0)
             & (keys <= queries)
             & (doc_of(keys) == doc_of(queries))
-            & (same | (opened == 1))
+            & ((column // BLK == PAD // BLK) | (line > 0.5))
         )
         bias[p] = jnp.where(allowed, 0.0, -1e30)
-        return carry
-
-    lax.fori_loop(0, pieces, mask_piece, 0)
 
     @pl.when(last)
     def _():
@@ -225,9 +224,6 @@
 
         lax.fori_loop(0, pieces, scale_piece, 0)
 
-    for copy in w_copies:
-        copy.wait()
-
     @pl.when(first)
     def _():
         for copy in tok_copies:
@@ -245,6 +241,8 @@
 
     @pl.when(jnp.logical_not(early))
     def _():
+        for copy in w_copies:
+            copy.wait()
         transpose_w()
 
     pl.semaphore_wait(barrier, n_dp + 1)
@@ -267,6 +265,10 @@
             @pl.when(sec > 0)
             def _():
                 arrival.wait_recv()
+
+            @pl.when(early & (p == 0))
+            def _():
+                w_copies[k].wait()
 
             values = xb[k, rows, :].astype(F32)
             squares = squares + fold_lanes(values * values)
@@ -321,33 +323,66 @@
         pltpu.make_async_copy(ref, ref, sem).wait()
 
     peers = []
-    for jx in range(KV_HEADS):
-        for jy in range(grid_y):
+    for jy in range(grid_y):
+        for jx in range(KV_HEADS):
             peer_x, peer_y = (x + jx) % KV_HEADS, (y + jy) % grid_y
-            peers.append((jx * grid_y + jy, peer_x * grid_y + peer_y, peer_x, peer_y))
+            peers.append((jy * KV_HEADS + jx, peer_x * grid_y + peer_y, peer_x, peer_y))
     others = pl.ds(1, n_dp - 1)
 
-    own_hidden = pltpu.make_async_copy(hb.at[x], hg.at[0], in_sem.at[0])
+    upper, lower = x * grid_y + (y + 1) % grid_y, x * grid_y + (y + grid_y - 1) % grid_y
+    half = seq_len // 2
+    far = grid_y - 1
+
+    own_hidden = pltpu.make_async_copy(hb.at[x], hg.at[0, 0], in_sem.at[0])
     own_hidden.start()
-    for j, dp, peer_x, peer_y in peers[1:]:
-        to_peer(dp, hb.at[peer_x], hg.at[j], h_send, h_recv).start()
+    for jx in range(1, KV_HEADS):
+        peer_x = (x + jx) % KV_HEADS
+        to_peer(peer_x * grid_y + y, hb.at[peer_x], hg.at[0, jx], hx_send, hx_recv).start()
+
+    def spread_h():
+        own_hidden.wait()
+        wait_for(hg.at[0, pl.ds(1, KV_HEADS - 1)], hx_recv)
+        if grid_y > 1:
+            to_peer(upper, hg.at[0], hg.at[1], hy_send.at[0], hy_recv.at[0]).start()
+            to_peer(lower, hg.at[0], hg.at[far], hy_send.at[1], hy_recv.at[1]).start()
+
+    def relay_h():
+        if grid_y > 1:
+            wait_for(hg.at[1], hy_recv.at[0])
+            wait_for(hg.at[far], hy_recv.at[1])
+            for i, (dp, source) in enumerate(((upper, 1), (lower, far))):
+                rows = pl.ds(i * half, half)
+                to_peer(
+                    dp, hg.at[source, :, rows], hg.at[2, :, rows], hr_send.at[i], hr_recv.at[i]
+                ).start()
 
     def transpose_h():
-        own_hidden.wait()
-        wait_for(hg.at[others], h_recv)
+        if grid_y > 1:
+            for i in range(2):
+                wait_for(hg.at[2, :, pl.ds(i * half, half)], hr_recv.at[i])
 
         def part(p, carry):
-            rows = pl.ds(pl.multiple_of(p * T, T), T)
+            rows = pl.ds(pl.multiple_of(p * span_rows, span_rows), span_rows)
             for c in range(CHUNK // 256):
-                hidden = hg[:, rows, pl.ds(c * 256, 256)].reshape(n_dp * T, 256)
+                hidden = hg[:, :, rows, pl.ds(c * 256, 256)].reshape(n_dp * span_rows, 256)
                 ht[p, pl.ds(c * 256, 256), :] = hidden.T
             return carry
 
-        lax.fori_loop(0, pieces, part, 0)
+        lax.fori_loop(0, pieces // SPAN, part, 0)
+
+    middle = sec < n_sec - 4
 
     @pl.when(early)
     def _():
         transpose_w()
+
+    @pl.when(early | middle)
+    def _():
+        spread_h()
+
+    @pl.when(early)
+    def _():
+        relay_h()
         transpose_h()
 
     def backward(step, carry):
@@ -394,17 +429,20 @@
             BF16
         )
         for c in range(grid_y):
-            do[p, c] = d_kv[:, c * cols : (c + 1) * cols]
+            do[p // SPAN, c, pl.ds(pl.multiple_of((p % SPAN) * T, T), T), :] = d_kv[
+                :, c * cols : (c + 1) * cols
+            ]
         inner = inner + fold_lanes(d_kv.astype(F32) * kvb[own, :].astype(F32))
         mean = jnp.sum(inner, -1, keepdims=True) / width
         inverse = rb[rows, :][:, :1]
 
         def send_d_kv():
-            dg[p, 0] = do[p, y]
+            q = p // SPAN
+            dg[q, 0] = do[q, y]
             for j, dp, peer_x, peer_y in peers[1:]:
-                to_peer(dp, do.at[p, peer_y], dg.at[p, j], d_send, d_recv.at[p]).start()
-
-        @pl.when(first)
+                to_peer(dp, do.at[q, peer_y], dg.at[q, j], d_send, d_recv.at[q]).start()
+
+        @pl.when(first & (p % SPAN == 0))
         def _():
             send_d_kv()
 
@@ -425,7 +463,7 @@
             d_hidden = dqb[k] + dot(d_kv, wt[k])
             normed = xb[k, rows, :].astype(F32) * inverse
             moment = d_hidden * normed
-            gsum[k] += moment[0:8] + moment[8:16] + moment[16:24] + moment[24:32]
+            gsum[k] += moment[0:8] + moment[8:16]
             d_inputs = inverse * (d_hidden * gf[k, 0:1, :] - normed * mean)
             go[k, rows, :] = (gb[k, rows, :].astype(F32) + d_inputs).astype(BF16)
             if k < 2:
@@ -433,9 +471,13 @@
             elif k == KV_HEADS - 1:
                 send_grads([k - 1, k])
 
-        @pl.when(sec > 0)
+        @pl.when((sec > 0) & (p % SPAN == 0))
         def _():
             send_d_kv()
+
+        @pl.when(jnp.logical_not(early | middle) & (step == pieces // 2 + 1))
+        def _():
+            spread_h()
 
         return carry
 
@@ -457,21 +499,22 @@
 
     @pl.when(jnp.logical_not(early))
     def _():
+        relay_h()
         transpose_h()
 
     def multiply(step, carry):
-        p = pieces - 1 - step
+        p = pieces // SPAN - 1 - step
         wait_for(dg.at[p, others], d_recv.at[p])
-        d_kv = dg[p].reshape(n_dp * T, cols)
+        d_kv = dg[p].reshape(n_dp * span_rows, cols)
         for c in range(CHUNK // 256):
             part = pl.ds(c * 256, 256)
             product = dot(ht[p, part, :], d_kv)
             wacc[part, :] = product + jnp.where(step > 0, wacc[part, :], 0.0)
         return carry
 
-    lax.fori_loop(0, pieces - 1, multiply, 0)
+    lax.fori_loop(0, pieces // SPAN - 1, multiply, 0)
     wait_for(dg.at[0, others], d_recv.at[0])
-    d_kv = dg[0].reshape(n_dp * T, cols)
+    d_kv = dg[0].reshape(n_dp * span_rows, cols)
     for jy in list(range(1, grid_y)) + [0]:
         peer_y = (y + jy) % grid_y
         part = pl.ds(pl.multiple_of(peer_y * block, block), block)
@@ -498,7 +541,10 @@
 
     if grid_y > 1:
         wait_for(eo.at[pl.ds(1, grid_y - 1)], e_send)
-    wait_for(hg.at[others], h_send)
+        for i in range(2):
+            wait_for(hg.at[0], hy_send.at[i])
+            wait_for(hg.at[2, :, pl.ds(i * half, half)], hr_send.at[i])
+    wait_for(hg.at[0, pl.ds(1, KV_HEADS - 1)], hx_send)
     wait_for(dg.at[:, others], d_send)
     wait_for(gg.at[others], s_send)
 
@@ -529,7 +575,7 @@
             jax.ShapeDtypeStruct((block, kv2), F32),
             jax.ShapeDtypeStruct((1, block), F32),
         ),
-        in_specs=[any_spec, any_spec, vmem, any_spec, smem, smem, smem],
+        in_specs=[any_spec, any_spec, vmem, any_spec, smem, smem, vmem],
         out_specs=(vmem, vmem),
         scratch_shapes=[
             pltpu.VMEM(features, BF16),
@@ -549,10 +595,10 @@
             pltpu.VMEM((KV_HEADS, 8, CHUNK), F32),
             pltpu.VMEM((KV_HEADS, 8, CHUNK), F32),
             pltpu.VMEM((KV_HEADS, 8, CHUNK), F32),
-            pltpu.VMEM((n_dp, seq_len, CHUNK), BF16),
-            pltpu.VMEM((pieces, CHUNK, n_dp * T), BF16),
-            pltpu.VMEM((pieces, grid_y, T, cols), BF16),
-            pltpu.VMEM((pieces, n_dp, T, cols), BF16),
+            pltpu.VMEM((grid_y, KV_HEADS, seq_len, CHUNK), BF16),
+            pltpu.VMEM((pieces // SPAN, CHUNK, n_dp * SPAN * T), BF16),
+            pltpu.VMEM((pieces // SPAN, grid_y, SPAN * T, cols), BF16),
+            pltpu.VMEM((pieces // SPAN, n_dp, SPAN * T, cols), BF16),
             pltpu.VMEM((CHUNK, cols), F32),
             pltpu.VMEM((grid_y, block, cols), BF16),
             pltpu.VMEM((grid_y, block, cols), BF16),
@@ -565,8 +611,12 @@
             dma((pieces, KV_HEADS)),
             dma,
             dma,
-            dma,
-            dma((pieces,)),
+            dma((2,)),
+            dma((2,)),
+            dma((2,)),
+            dma((2,)),
+            dma,
+            dma((pieces // SPAN,)),
             dma,
             dma((grid_y,)),
             dma,

time: 218 us -> 211 us (0.968)
  the two profiles are of different devices: /device:TPU:229 before, /device:TPU:2 now
where the time goes in v3:
time: 211 us; the launch traced here: 207 us
  Pallas kernels  203 us (96%)
  local copies, waits for them, and re-layouts  4.16 us (2%)
    pallas_call x1, Pallas kernels, local(): pl.pallas_call(functools.partial(kernel, n_sec, n_dp), out_shape=(jax.Sha...  203 us

profile of v3, /device:TPU:2, one launch (start us, length us, event | category | flops | bytes accessed | tf_op | source)
XLA Modules:
  0.0 207.3 jit_solution(13811970893033068808)
XLA Ops:
  0.6 1.3 copy.9.table
  1.9 202.5 %relay.1 = (f32[256,1024]{1,0:T(8,128)}, f32[1,256]{1,0:T(1,128)}) custom-call(bf16[1,192,4096]{2,1,0:T(8,128)(2,1)} %tok.1, bf16[1,192,4096]{2,1,0:T(8,128)(2,1)} %ups.1, bf16[1,4096]{1,0:T(2,128)(2,1)} %gain.1, bf16[1,4096,1024]{2,1,0:T(8,128)(2,1)} %w.1, s32[1,4]{1,0:T(1,128)} %docs.1, s32[1,4]{1,0:T(1,128)} %segs.1, s32[1,12,12]{2,1,0:T(8,128)} %copy.9.table), custom_call_target="tpu_custom_call" | custom-call | flops 7000000000 | bytes 12582912 | tf_op jit(solution)/shard_map/relay/pallas_call | solution.py:572
  204.4 0.0 copy-start
  204.5 2.3 %copy.12 = f32[1,256,1024]{2,1,0:T(8,128)} copy(f32[1,256,1024]{2,1,0:T(8,128)} %bitcast.1) | data formatting | bytes 2097152
  206.8 0.0 copy-done
  206.8 0.6 copy.13
Async XLA Ops:
  204.4 2.3 %copy-start = (f32[1,256]{1,0:T(1,128)S(1)}, f32[1,256]{1,0:T(1,128)}, u32[]{:S(2)}) copy-start(f32[1,256]{1,0:T(1,128)} %get-tuple-element.9) | copy-start | bytes 3076

commit v4 on v3

--- a/solution.py
+++ b/solution.py
@@ -155,10 +155,15 @@
             copy.start()
 
     barrier = pltpu.get_barrier_semaphore()
-    for neighbour in ((sec + 1) % n_sec, (sec + n_sec - 1) % n_sec):
-        pl.semaphore_signal(
-            barrier, inc=1, device_id={"section": neighbour}, device_id_type=MESH
-        )
+
+    @pl.when(sec > 0)
+    def _():
+        pl.semaphore_signal(barrier, inc=1, device_id={"section": sec - 1}, device_id_type=MESH)
+
+    @pl.when(sec < n_sec - 1)
+    def _():
+        pl.semaphore_signal(barrier, inc=1, device_id={"section": sec + 1}, device_id_type=MESH)
+
     for j in range(1, n_dp):
         pl.semaphore_signal(
             barrier, inc=1, device_id={"dp": (me + j) % n_dp}, device_id_type=MESH
@@ -186,7 +191,7 @@
     column = lax.broadcasted_iota(jnp.int32, (T, WINDOW), 1)
 
     blocks = seq_len // BLK
-    opened = table[0].astype(BF16)
+    opened = table[:, 0, :].astype(BF16)
     block_row = lax.broadcasted_iota(jnp.int32, (blocks, WINDOW), 0)
     block_column = lax.broadcasted_iota(jnp.int32, (blocks, WINDOW), 1) // BLK
     for p in range(pieces):
@@ -245,7 +250,8 @@
             copy.wait()
         transpose_w()
 
-    pl.semaphore_wait(barrier, n_dp + 1)
+    before, after = (sec + n_sec - 1) // n_sec, (2 * n_sec - 2 - sec) // n_sec
+    pl.semaphore_wait(barrier, n_dp - 1 + before + after)
 
     def forward(p, carry):
         start = pl.multiple_of(p * T, T)
@@ -370,7 +376,11 @@
 
         lax.fori_loop(0, pieces // SPAN, part, 0)
 
-    middle = sec < n_sec - 4
+    late = jnp.logical_not(early) & (sec >= n_sec - 3)
+    middle = jnp.logical_not(early | late)
+    base = 3 * n_sec // 8
+    relay_turn = 2 * (sec - base)
+    late_turn = 2 * pieces // 3 - 3 * (n_sec - 1 - sec)
 
     @pl.when(early)
     def _():
@@ -391,6 +401,8 @@
         rows = pl.ds(start, T)
         window = pl.ds(start, WINDOW)
         own = pl.ds(pl.multiple_of(start + PAD, T), T)
+        previous = pl.ds(start, PAD)
+        own_keys, own_vals = [], []
         inner = jnp.zeros((T, 128), F32)
         for k in range(KV_HEADS):
             if k % 2 == 0:
@@ -423,11 +435,15 @@
             d_query = to_lanes(dot(d_low, keys))
             dqb[k] = d_query
             inner = inner + fold_lanes(d_query * hidden.astype(F32))
-            dacc[k, window, :] += dot(d_low_t, query)
-            dacc[KV_HEADS + k, window, :] += dot(probs_t.astype(BF16), grads)
-        d_kv = jnp.concatenate([dacc[i, own, :] for i in range(2 * KV_HEADS)], axis=1).astype(
-            BF16
-        )
+            d_vals = dot(probs_t.astype(BF16), grads)
+            d_keys = dot(d_low_t, query)
+            own_vals.append(dacc[KV_HEADS + k, own, :] + d_vals[PAD:])
+            own_keys.append(dacc[k, own, :] + d_keys[PAD:])
+            dacc[KV_HEADS + k, previous, :] += d_vals[:PAD]
+            dacc[k, previous, :] += d_keys[:PAD]
+        d_keys = jnp.concatenate(own_keys, axis=1).astype(BF16)
+        d_vals = jnp.concatenate(own_vals, axis=1).astype(BF16)
+        d_kv = jnp.concatenate([d_keys, d_vals], axis=1)
         for c in range(grid_y):
             do[p // SPAN, c, pl.ds(pl.multiple_of((p % SPAN) * T, T), T), :] = d_kv[
                 :, c * cols : (c + 1) * cols
@@ -441,10 +457,6 @@
             dg[q, 0] = do[q, y]
             for j, dp, peer_x, peer_y in peers[1:]:
                 to_peer(dp, do.at[q, peer_y], dg.at[q, j], d_send, d_recv.at[q]).start()
-
-        @pl.when(first & (p % SPAN == 0))
-        def _():
-            send_d_kv()
 
         def send_grads(chunks):
             @pl.when(sec > 0)
@@ -460,12 +472,19 @@
                     ).start()
 
         for k in range(KV_HEADS):
-            d_hidden = dqb[k] + dot(d_kv, wt[k])
+            d_hidden = dot(d_vals, wt[k, pl.ds(kv_width, kv_width), :]) + dqb[k]
+            d_hidden = d_hidden + dot(d_keys, wt[k, pl.ds(0, kv_width), :])
             normed = xb[k, rows, :].astype(F32) * inverse
             moment = d_hidden * normed
             gsum[k] += moment[0:8] + moment[8:16]
             d_inputs = inverse * (d_hidden * gf[k, 0:1, :] - normed * mean)
             go[k, rows, :] = (gb[k, rows, :].astype(F32) + d_inputs).astype(BF16)
+            if k == 0:
+
+                @pl.when(first & (p % SPAN == 0))
+                def _():
+                    send_d_kv()
+
             if k < 2:
                 send_grads([k])
             elif k == KV_HEADS - 1:
@@ -475,9 +494,20 @@
         def _():
             send_d_kv()
 
-        @pl.when(jnp.logical_not(early | middle) & (step == pieces // 2 + 1))
+        @pl.when(late & (step == late_turn))
         def _():
             spread_h()
+
+        @pl.when(
+            middle
+            & (
+                (step == relay_turn)
+                | ((step == 0) & (relay_turn < 0))
+                | ((step == pieces - 1) & (relay_turn >= pieces))
+            )
+        )
+        def _():
+            relay_h()
 
         return carry
 
@@ -497,9 +527,12 @@
     for j, dp, peer_x, peer_y in peers[1:]:
         to_peer(dp, gain_block(dp), gg.at[j], s_send, s_recv).start()
 
+    @pl.when(late)
+    def _():
+        relay_h()
+
     @pl.when(jnp.logical_not(early))
     def _():
-        relay_h()
         transpose_h()
 
     def multiply(step, carry):
@@ -623,13 +656,13 @@
             dma,
         ],
         compiler_params=pltpu.CompilerParams(
-            collective_id=0, has_side_effects=True, vmem_limit_bytes=60 * 1024 * 1024
+            collective_id=0, has_side_effects=True, vmem_limit_bytes=52 * 1024 * 1024
         ),
         cost_estimate=pl.CostEstimate(
             flops=7 * 10**9, bytes_accessed=12 * 2**20, transcendentals=10**6
         ),
         name="relay",
-    )(tokens, upstream, gains, w_kv, doc_lengths, seg_lengths, block_mask)
+    )(tokens, upstream, gains, w_kv, doc_lengths, seg_lengths, block_mask.transpose(1, 0, 2))
     return grad_weight[None], grad_gain
 
 

time: 211 us -> 204 us (0.967); the launches traced: 207 us -> 204 us
  Pallas kernels: 203 us -> 199 us
    pallas_call x1, Pallas kernels: 203 us -> 199 us  [local(): pl.pallas_call(functools.partial(kernel, n_sec, n_dp), out_shape=(jax.Sha...]
    unnamed x5 -> x10, local copies, waits for them, and re-layouts: 4.16 us -> 4.25 us
where the time goes in v4:
time: 204 us
  Pallas kernels  199 us (98%)
  local copies, waits for them, and re-layouts  4.25 us (2%)
    pallas_call x1, Pallas kernels, local(): pl.pallas_call(functools.partial(kernel, n_sec, n_dp), out_shape=(jax.Sha...  199 us
    unnamed x10, local copies, waits for them, and re-layouts  4.25 us

profile of v4, /device:TPU:2, one launch (start us, length us, event | category | flops | bytes accessed | tf_op | source)
XLA Modules:
  0.0 204.0 jit_solution(9503818373993954042)
XLA Ops:
  0.6 0.0 copy-start
  0.6 0.7 copy-done
  1.4 0.0 copy-start.1
  1.4 0.7 copy-done.1
  2.0 0.0 copy-start.2
  2.0 0.7 copy-done.2
  2.7 0.0 copy-start.3
  2.7 0.7 copy-done.3
  3.4 199.1 %relay.1 = (f32[256,1024]{1,0:T(8,128)S(1)}, f32[1,256]{1,0:T(1,128)S(1)}) custom-call(bf16[1,192,4096]{2,1,0:T(8,128)(2,1)} %tok.1, bf16[1,192,4096]{2,1,0:T(8,128)(2,1)} %ups.1, bf16[1,4096]{1,0:T(2,128)(2,1)S(1)} %copy-done, bf16[1,4096,1024]{2,1,0:T(8,128)(2,1)} %w.1, s32[1,4]{1,0:T(1,128)S(1)} %copy-done.2, s32[1,4]{1,0:T(1,128)S(1)} %copy-done.3, ...), custom_call_target="tpu_custom_call" | custom-call | flops 7000000000 | bytes 12582912 | tf_op jit(solution)/shard_map/relay/pallas_call | solution.py:605
  202.5 1.0 copy.11
  203.5 0.6 copy.12
Async XLA Ops:
  0.6 0.7 copy-start
  1.4 0.7 copy-start.1
  2.0 0.7 copy-start.2
  2.7 0.7 copy-start.3

commit v5 on v4

--- a/solution.py
+++ b/solution.py
@@ -76,8 +76,10 @@
     go,
     wb,
     wt,
-    kvb,
-    dacc,
+    kb,
+    vb,
+    dk_acc,
+    dv_acc,
     pb,
     pt,
     dqb,
@@ -169,8 +171,10 @@
             barrier, inc=1, device_id={"dp": (me + j) % n_dp}, device_id_type=MESH
         )
 
-    kvb[pl.ds(0, PAD), :] = jnp.zeros((PAD, 2 * kv_width), BF16)
-    dacc[...] = jnp.zeros_like(dacc)
+    kb[pl.ds(0, PAD), :] = jnp.zeros((PAD, kv_width), BF16)
+    vb[pl.ds(0, PAD), :] = jnp.zeros((PAD, kv_width), BF16)
+    dk_acc[...] = jnp.zeros_like(dk_acc)
+    dv_acc[...] = jnp.zeros_like(dv_acc)
     gsum[...] = jnp.zeros_like(gsum)
     for k in range(KV_HEADS):
         gf[k] = jnp.broadcast_to(
@@ -256,7 +260,10 @@
     def forward(p, carry):
         start = pl.multiple_of(p * T, T)
         rows = pl.ds(start, T)
-        acc = jnp.zeros((T, 2 * kv_width), F32)
+        keys_part, vals_part = pl.ds(0, kv_width), pl.ds(kv_width, kv_width)
+        new_keys = jnp.zeros((T, kv_width), F32)
+        new_vals = jnp.zeros((T, kv_width), F32)
+        scaled = []
         squares = jnp.zeros((T, 128), F32)
         for k in range(KV_HEADS):
             arrival = pltpu.make_async_remote_copy(
@@ -278,23 +285,33 @@
 
             values = xb[k, rows, :].astype(F32)
             squares = squares + fold_lanes(values * values)
-            acc = acc + dot((values * gf[k, 0:1, :]).astype(BF16), wb[k])
+            scaled.append((values * gf[k, 0:1, :]).astype(BF16))
+            new_keys = new_keys + dot(scaled[k], wb[k, :, keys_part])
+            if k > 0:
+                new_vals = new_vals + dot(scaled[k - 1], wb[k - 1, :, vals_part])
         inverse = lax.rsqrt(jnp.sum(squares, -1, keepdims=True) / width + EPSILON)
         rb[rows, :] = jnp.broadcast_to(inverse, (T, 128))
-        kvb[pl.ds(pl.multiple_of(start + PAD, T), T), :] = (acc * inverse).astype(BF16)
+        own = pl.ds(pl.multiple_of(start + PAD, T), T)
         window = pl.ds(start, WINDOW)
+        kb[own, :] = (new_keys * inverse).astype(BF16)
         bias_rows = jnp.concatenate([bias[p]] * GROUP, axis=0)
+        raws = []
         for k in range(KV_HEADS):
             values = xb[k, rows, :].astype(F32)
             hidden = (values * inverse * gf[k, 0:1, :]).astype(BF16)
             hb[k, rows, :] = hidden
-            keys = kvb[window, pl.ds(k * HEAD_DIM, HEAD_DIM)]
-            vals = kvb[window, pl.ds(kv_width + k * HEAD_DIM, HEAD_DIM)]
+            keys = kb[window, pl.ds(k * HEAD_DIM, HEAD_DIM)]
             scores = dot_t(to_rows(hidden), keys)
-            raw = jnp.exp2(scores * EXP_SCALE + bias_rows)
+            raws.append(jnp.exp2(scores * EXP_SCALE + bias_rows))
+        last_k = KV_HEADS - 1
+        new_vals = new_vals + dot(scaled[last_k], wb[last_k, :, vals_part])
+        vb[own, :] = (new_vals * inverse).astype(BF16)
+        for k in range(KV_HEADS):
+            raw = raws[k]
+            vals = vb[window, pl.ds(k * HEAD_DIM, HEAD_DIM)]
             share = 1.0 / jnp.sum(raw, -1, keepdims=True)
             mixed = dot(raw.astype(BF16), vals) * share
-            xo[k, rows, :] = (values + to_lanes(mixed)).astype(BF16)
+            xo[k, rows, :] = (xb[k, rows, :].astype(F32) + to_lanes(mixed)).astype(BF16)
             probs = raw * share
             pb[p, k] = probs
             pt[p, k] = probs.T
@@ -403,44 +420,56 @@
         own = pl.ds(pl.multiple_of(start + PAD, T), T)
         previous = pl.ds(start, PAD)
         own_keys, own_vals = [], []
+        partial = [0.0] * KV_HEADS
         inner = jnp.zeros((T, 128), F32)
-        for k in range(KV_HEADS):
-            if k % 2 == 0:
-
-                @pl.when(sec < n_sec - 1)
-                def _():
-                    for i in (k, k + 1):
-                        pltpu.make_async_remote_copy(
-                            src_ref=gb.at[i, rows],
-                            dst_ref=gb.at[i, rows],
-                            send_sem=g_send,
-                            recv_sem=g_recv.at[p, i],
-                            device_id={"section": sec},
-                            device_id_type=MESH,
-                        ).wait_recv()
-
-            grads = to_rows(gb[k, rows, :])
-            hidden = hb[k, rows, :]
-            query = to_rows(hidden)
-            keys = kvb[window, pl.ds(k * HEAD_DIM, HEAD_DIM)]
-            vals = kvb[window, pl.ds(kv_width + k * HEAD_DIM, HEAD_DIM)]
-            probs = pb[p, k]
-            product = probs * dot_t(grads, vals)
-            total = jnp.sum(product, -1, keepdims=True)
-            d_low = ((product - probs * total) * SCALE).astype(BF16)
-            probs_t = pt[p, k]
-            product_t = probs_t * dot_t(vals, grads)
-            total_t = jnp.sum(product_t, 0, keepdims=True)
-            d_low_t = ((product_t - probs_t * total_t) * SCALE).astype(BF16)
-            d_query = to_lanes(dot(d_low, keys))
-            dqb[k] = d_query
-            inner = inner + fold_lanes(d_query * hidden.astype(F32))
-            d_vals = dot(probs_t.astype(BF16), grads)
-            d_keys = dot(d_low_t, query)
-            own_vals.append(dacc[KV_HEADS + k, own, :] + d_vals[PAD:])
-            own_keys.append(dacc[k, own, :] + d_keys[PAD:])
-            dacc[KV_HEADS + k, previous, :] += d_vals[:PAD]
-            dacc[k, previous, :] += d_keys[:PAD]
+        for pair in range(KV_HEADS // 2):
+            heads = (2 * pair, 2 * pair + 1)
+
+            @pl.when(sec < n_sec - 1)
+            def _():
+                for i in heads:
+                    pltpu.make_async_remote_copy(
+                        src_ref=gb.at[i, rows],
+                        dst_ref=gb.at[i, rows],
+                        send_sem=g_send,
+                        recv_sem=g_recv.at[p, i],
+                        device_id={"section": sec},
+                        device_id_type=MESH,
+                    ).wait_recv()
+
+            grads, d_vals = {}, {}
+            for k in heads:
+                grads[k] = to_rows(gb[k, rows, :])
+                d_vals[k] = dot(pt[p, k].astype(BF16), grads[k])
+                own_vals.append(dv_acc[k, own, :] + d_vals[k][PAD:])
+            pair_vals = jnp.concatenate(own_vals[-2:], axis=1).astype(BF16)
+            d_probs, d_probs_t = {}, {}
+            for k in heads:
+                vals = vb[window, pl.ds(k * HEAD_DIM, HEAD_DIM)]
+                d_probs[k] = dot_t(grads[k], vals)
+                d_probs_t[k] = dot_t(vals, grads[k])
+            part = pl.ds(kv_width + pair * 2 * HEAD_DIM, 2 * HEAD_DIM)
+            for c in range(KV_HEADS):
+                partial[c] = partial[c] + dot(pair_vals, wt[c, part, :])
+            for k in heads:
+                hidden = hb[k, rows, :]
+                query = to_rows(hidden)
+                keys = kb[window, pl.ds(k * HEAD_DIM, HEAD_DIM)]
+                probs = pb[p, k]
+                product = probs * d_probs[k]
+                total = jnp.sum(product, -1, keepdims=True)
+                d_low = ((product - probs * total) * SCALE).astype(BF16)
+                probs_t = pt[p, k]
+                product_t = probs_t * d_probs_t[k]
+                total_t = jnp.sum(product_t, 0, keepdims=True)
+                d_low_t = ((product_t - probs_t * total_t) * SCALE).astype(BF16)
+                d_keys = dot(d_low_t, query)
+                own_keys.append(dk_acc[k, own, :] + d_keys[PAD:])
+                d_query = to_lanes(dot(d_low, keys))
+                dqb[k] = d_query
+                inner = inner + fold_lanes(d_query * hidden.astype(F32))
+                dk_acc[k, previous, :] += d_keys[:PAD]
+                dv_acc[k, previous, :] += d_vals[k][:PAD]
         d_keys = jnp.concatenate(own_keys, axis=1).astype(BF16)
         d_vals = jnp.concatenate(own_vals, axis=1).astype(BF16)
         d_kv = jnp.concatenate([d_keys, d_vals], axis=1)
@@ -448,15 +477,18 @@
             do[p // SPAN, c, pl.ds(pl.multiple_of((p % SPAN) * T, T), T), :] = d_kv[
                 :, c * cols : (c + 1) * cols
             ]
-        inner = inner + fold_lanes(d_kv.astype(F32) * kvb[own, :].astype(F32))
+        inner = inner + fold_lanes(d_keys.astype(F32) * kb[own, :].astype(F32))
+        inner = inner + fold_lanes(d_vals.astype(F32) * vb[own, :].astype(F32))
         mean = jnp.sum(inner, -1, keepdims=True) / width
         inverse = rb[rows, :][:, :1]
 
-        def send_d_kv():
+        def send_d_kv(part):
             q = p // SPAN
-            dg[q, 0] = do[q, y]
+            dg[q, 0, part] = do[q, y, part]
             for j, dp, peer_x, peer_y in peers[1:]:
-                to_peer(dp, do.at[q, peer_y], dg.at[q, j], d_send, d_recv.at[q]).start()
+                to_peer(
+                    dp, do.at[q, peer_y, part], dg.at[q, j, part], d_send, d_recv.at[q]
+                ).start()
 
         def send_grads(chunks):
             @pl.when(sec > 0)
@@ -472,8 +504,7 @@
                     ).start()
 
         for k in range(KV_HEADS):
-            d_hidden = dot(d_vals, wt[k, pl.ds(kv_width, kv_width), :]) + dqb[k]
-            d_hidden = d_hidden + dot(d_keys, wt[k, pl.ds(0, kv_width), :])
+            d_hidden = partial[k] + dqb[k] + dot(d_keys, wt[k, pl.ds(0, kv_width), :])
             normed = xb[k, rows, :].astype(F32) * inverse
             moment = d_hidden * normed
             gsum[k] += moment[0:8] + moment[8:16]
@@ -481,9 +512,9 @@
             go[k, rows, :] = (gb[k, rows, :].astype(F32) + d_inputs).astype(BF16)
             if k == 0:
 
-                @pl.when(first & (p % SPAN == 0))
+                @pl.when(first)
                 def _():
-                    send_d_kv()
+                    send_d_kv(pl.ds(pl.multiple_of((p % SPAN) * T, T), T))
 
             if k < 2:
                 send_grads([k])
@@ -492,7 +523,7 @@
 
         @pl.when((sec > 0) & (p % SPAN == 0))
         def _():
-            send_d_kv()
+            send_d_kv(pl.ds(0, span_rows))
 
         @pl.when(late & (step == late_turn))
         def _():
@@ -618,8 +649,10 @@
             pltpu.VMEM(features, BF16),
             pltpu.VMEM((KV_HEADS, CHUNK, kv2), BF16),
             pltpu.VMEM((KV_HEADS, kv2, CHUNK), BF16),
-            pltpu.VMEM((PAD + seq_len, kv2), BF16),
-            pltpu.VMEM((2 * KV_HEADS, PAD + seq_len, HEAD_DIM), F32),
+            pltpu.VMEM((PAD + seq_len, kv2 // 2), BF16),
+            pltpu.VMEM((PAD + seq_len, kv2 // 2), BF16),
+            pltpu.VMEM((KV_HEADS, PAD + seq_len, HEAD_DIM), F32),
+            pltpu.VMEM((KV_HEADS, PAD + seq_len, HEAD_DIM), F32),
             pltpu.VMEM((pieces, KV_HEADS, GROUP * T, WINDOW), F32),
             pltpu.VMEM((pieces, KV_HEADS, WINDOW, GROUP * T), F32),
             pltpu.VMEM((KV_HEADS, T, CHUNK), F32),
@@ -656,7 +689,7 @@
             dma,
         ],
         compiler_params=pltpu.CompilerParams(
-            collective_id=0, has_side_effects=True, vmem_limit_bytes=52 * 1024 * 1024
+            collective_id=0, has_side_effects=True, vmem_limit_bytes=60 * 1024 * 1024
         ),
         cost_estimate=pl.CostEstimate(
             flops=7 * 10**9, bytes_accessed=12 * 2**20, transcendentals=10**6

time: 204 us -> 192 us (0.941)
  Pallas kernels: 199 us -> 188 us
    pallas_call x1, Pallas kernels: 199 us -> 188 us  [local(): pl.pallas_call(functools.partial(kernel, n_sec, n_dp), out_shape=(jax.Sha...]
    unnamed x10 -> x4, local copies, waits for them, and re-layouts: 4.25 us -> 2.87 us
where the time goes in v5:
time: 192 us; the launch traced here: 191 us
  Pallas kernels  188 us (98%)
  local copies, waits for them, and re-layouts  2.87 us (1%)
    pallas_call x1, Pallas kernels, local(): pl.pallas_call(functools.partial(kernel, n_sec, n_dp), out_shape=(jax.Sha...  188 us

profile of v5, /device:TPU:2, one launch (start us, length us, event | category | flops | bytes accessed | tf_op | source)
XLA Modules:
  0.0 191.3 jit_solution(6202527322516384062)
XLA Ops:
  0.6 187.8 %relay.1 = (f32[256,1024]{1,0:T(8,128)}, f32[1,256]{1,0:T(1,128)}) custom-call(bf16[1,192,4096]{2,1,0:T(8,128)(2,1)} %tok.1, bf16[1,192,4096]{2,1,0:T(8,128)(2,1)} %ups.1, bf16[1,4096]{1,0:T(2,128)(2,1)} %gain.1, bf16[1,4096,1024]{2,1,0:T(8,128)(2,1)} %w.1, s32[1,4]{1,0:T(1,128)} %docs.1, s32[1,4]{1,0:T(1,128)} %segs.1, s32[12,1,12]{2,1,0:T(1,128)} %bitcast.3), custom_call_target="tpu_custom_call" | custom-call | flops 7000000000 | bytes 12582912 | tf_op jit(solution)/shard_map/relay/pallas_call | solution.py:636
  188.4 0.0 copy-start
  188.4 2.3 %copy.11 = f32[1,256,1024]{2,1,0:T(8,128)} copy(f32[1,256,1024]{2,1,0:T(8,128)} %bitcast.2) | data formatting | bytes 2097152
  190.7 0.0 copy-done
  190.8 0.6 copy.12
Async XLA Ops:
  188.4 2.3 %copy-start = (f32[1,256]{1,0:T(1,128)S(1)}, f32[1,256]{1,0:T(1,128)}, u32[]{:S(2)}) copy-start(f32[1,256]{1,0:T(1,128)} %get-tuple-element.9) | copy-start | bytes 3076

commit v6 on v5

--- a/solution.py
+++ b/solution.py
@@ -17,7 +17,7 @@
 EPSILON = 1e-06
 
 T = 16
-SPAN = 2
+SPAN = 4
 WINDOW = 128
 PAD = WINDOW - T
 CHUNK = GROUP * HEAD_DIM
@@ -255,7 +255,6 @@
         transpose_w()
 
     before, after = (sec + n_sec - 1) // n_sec, (2 * n_sec - 2 - sec) // n_sec
-    pl.semaphore_wait(barrier, n_dp - 1 + before + after)
 
     def forward(p, carry):
         start = pl.multiple_of(p * T, T)
@@ -315,6 +314,10 @@
             probs = raw * share
             pb[p, k] = probs
             pt[p, k] = probs.T
+
+        @pl.when(p == 0)
+        def _():
+            pl.semaphore_wait(barrier, n_dp - 1 + before + after)
 
         @pl.when(sec < n_sec - 1)
         def _():
@@ -490,6 +493,21 @@
                     dp, do.at[q, peer_y, part], dg.at[q, j, part], d_send, d_recv.at[q]
                 ).start()
 
+        def send_parts():
+            near = sec < 2
+
+            @pl.when((p % SPAN == 0) & jnp.logical_not(near & (p == 0)))
+            def _():
+                send_d_kv(pl.ds(0, span_rows))
+
+            @pl.when(near & (p == 1))
+            def _():
+                send_d_kv(pl.ds(T, span_rows - T))
+
+            @pl.when(near & (p == 0))
+            def _():
+                send_d_kv(pl.ds(0, T))
+
         def send_grads(chunks):
             @pl.when(sec > 0)
             def _():
@@ -514,16 +532,16 @@
 
                 @pl.when(first)
                 def _():
-                    send_d_kv(pl.ds(pl.multiple_of((p % SPAN) * T, T), T))
+                    send_parts()
 
             if k < 2:
                 send_grads([k])
             elif k == KV_HEADS - 1:
                 send_grads([k - 1, k])
 
-        @pl.when((sec > 0) & (p % SPAN == 0))
+        @pl.when(sec > 0)
         def _():
-            send_d_kv(pl.ds(0, span_rows))
+            send_parts()
 
         @pl.when(late & (step == late_turn))
         def _():
@@ -549,14 +567,6 @@
         return gs.at[
             column // CHUNK, :, pl.ds(pl.multiple_of(column % CHUNK, block), block)
         ]
-
-    for k in range(KV_HEADS):
-        total = jnp.sum(gsum[k], 0, keepdims=True).astype(BF16).astype(F32)
-        gs[k] = jnp.broadcast_to(total, (8, CHUNK))
-    own_gain = pltpu.make_async_copy(gain_block(me), gg.at[0], in_sem.at[1])
-    own_gain.start()
-    for j, dp, peer_x, peer_y in peers[1:]:
-        to_peer(dp, gain_block(dp), gg.at[j], s_send, s_recv).start()
 
     @pl.when(late)
     def _():
@@ -590,6 +600,14 @@
             to_peer(
                 x * grid_y + peer_y, eo.at[jy], eg.at[jy], e_send, e_recv.at[jy]
             ).start()
+
+    for k in range(KV_HEADS):
+        total = jnp.sum(gsum[k], 0, keepdims=True).astype(BF16).astype(F32)
+        gs[k] = jnp.broadcast_to(total, (8, CHUNK))
+    own_gain = pltpu.make_async_copy(gain_block(me), gg.at[0], in_sem.at[1])
+    own_gain.start()
+    for j, dp, peer_x, peer_y in peers[1:]:
+        to_peer(dp, gain_block(dp), gg.at[j], s_send, s_recv).start()
 
     own_gain.wait()
     wait_for(gg.at[others], s_recv)

time: 192 us -> 190 us (0.990)
  Pallas kernels: 188 us -> 186 us
where the time goes in v6:
time: 190 us
  Pallas kernels  186 us (98%)
  local copies, waits for them, and re-layouts  2.87 us (2%)
    pallas_call x1, Pallas kernels, local(): pl.pallas_call(functools.partial(kernel, n_sec, n_dp), out_shape=(jax.Sha...  186 us

profile of v6, /device:TPU:2, one launch (start us, length us, event | category | flops | bytes accessed | tf_op | source)
XLA Modules:
  0.0 189.7 jit_solution(16004627520527873841)
XLA Ops:
  0.6 186.2 %relay.1 = (f32[256,1024]{1,0:T(8,128)}, f32[1,256]{1,0:T(1,128)}) custom-call(bf16[1,192,4096]{2,1,0:T(8,128)(2,1)} %tok.1, bf16[1,192,4096]{2,1,0:T(8,128)(2,1)} %ups.1, bf16[1,4096]{1,0:T(2,128)(2,1)} %gain.1, bf16[1,4096,1024]{2,1,0:T(8,128)(2,1)} %w.1, s32[1,4]{1,0:T(1,128)} %docs.1, s32[1,4]{1,0:T(1,128)} %segs.1, s32[12,1,12]{2,1,0:T(1,128)} %bitcast.3), custom_call_target="tpu_custom_call" | custom-call | flops 7000000000 | bytes 12582912 | tf_op jit(solution)/shard_map/relay/pallas_call | solution.py:654
  186.9 0.0 copy-start
  186.9 2.3 %copy.11 = f32[1,256,1024]{2,1,0:T(8,128)} copy(f32[1,256,1024]{2,1,0:T(8,128)} %bitcast.2) | data formatting | bytes 2097152
  189.2 0.0 copy-done
  189.2 0.6 copy.12
Async XLA Ops:
  186.9 2.3 %copy-start = (f32[1,256]{1,0:T(1,128)S(1)}, f32[1,256]{1,0:T(1,128)}, u32[]{:S(2)}) copy-start(f32[1,256]{1,0:T(1,128)} %get-tuple-element.9) | copy-start | bytes 3076

commit v7 on v6

--- a/solution.py
+++ b/solution.py
@@ -265,22 +265,24 @@
         scaled = []
         squares = jnp.zeros((T, 128), F32)
         for k in range(KV_HEADS):
-            arrival = pltpu.make_async_remote_copy(
-                src_ref=xb.at[k, rows],
-                dst_ref=xb.at[k, rows],
-                send_sem=f_send,
-                recv_sem=f_recv.at[p, k],
-                device_id={"section": sec},
-                device_id_type=MESH,
-            )
-
-            @pl.when(sec > 0)
-            def _():
-                arrival.wait_recv()
-
-            @pl.when(early & (p == 0))
-            def _():
-                w_copies[k].wait()
+            if k % 2 == 0:
+                arrival = pltpu.make_async_remote_copy(
+                    src_ref=xb.at[pl.ds(k, 2), rows],
+                    dst_ref=xb.at[pl.ds(k, 2), rows],
+                    send_sem=f_send,
+                    recv_sem=f_recv.at[p, k // 2],
+                    device_id={"section": sec},
+                    device_id_type=MESH,
+                )
+
+                @pl.when(sec > 0)
+                def _():
+                    arrival.wait_recv()
+
+                @pl.when(early & (p == 0))
+                def _():
+                    w_copies[k].wait()
+                    w_copies[k + 1].wait()
 
             values = xb[k, rows, :].astype(F32)
             squares = squares + fold_lanes(values * values)
@@ -321,12 +323,12 @@
 
         @pl.when(sec < n_sec - 1)
         def _():
-            for k in range(KV_HEADS):
+            for i in range(KV_HEADS // 2):
                 pltpu.make_async_remote_copy(
-                    src_ref=xo.at[k, rows],
-                    dst_ref=xb.at[k, rows],
+                    src_ref=xo.at[pl.ds(2 * i, 2), rows],
+                    dst_ref=xb.at[pl.ds(2 * i, 2), rows],
                     send_sem=f_send,
-                    recv_sem=f_recv.at[p, k],
+                    recv_sem=f_recv.at[p, i],
                     device_id={"section": sec + 1},
                     device_id_type=MESH,
                 ).start()
@@ -430,15 +432,14 @@
 
             @pl.when(sec < n_sec - 1)
             def _():
-                for i in heads:
-                    pltpu.make_async_remote_copy(
-                        src_ref=gb.at[i, rows],
-                        dst_ref=gb.at[i, rows],
-                        send_sem=g_send,
-                        recv_sem=g_recv.at[p, i],
-                        device_id={"section": sec},
-                        device_id_type=MESH,
-                    ).wait_recv()
+                pltpu.make_async_remote_copy(
+                    src_ref=gb.at[pl.ds(2 * pair, 2), rows],
+                    dst_ref=gb.at[pl.ds(2 * pair, 2), rows],
+                    send_sem=g_send,
+                    recv_sem=g_recv.at[p, pair],
+                    device_id={"section": sec},
+                    device_id_type=MESH,
+                ).wait_recv()
 
             grads, d_vals = {}, {}
             for k in heads:
@@ -508,18 +509,17 @@
             def _():
                 send_d_kv(pl.ds(0, T))
 
-        def send_grads(chunks):
+        def send_grads(pair):
             @pl.when(sec > 0)
             def _():
-                for k in chunks:
-                    pltpu.make_async_remote_copy(
-                        src_ref=go.at[k, rows],
-                        dst_ref=gb.at[k, rows],
-                        send_sem=g_send,
-                        recv_sem=g_recv.at[p, k],
-                        device_id={"section": sec - 1},
-                        device_id_type=MESH,
-                    ).start()
+                pltpu.make_async_remote_copy(
+                    src_ref=go.at[pl.ds(2 * pair, 2), rows],
+                    dst_ref=gb.at[pl.ds(2 * pair, 2), rows],
+                    send_sem=g_send,
+                    recv_sem=g_recv.at[p, pair],
+                    device_id={"section": sec - 1},
+                    device_id_type=MESH,
+                ).start()
 
         for k in range(KV_HEADS):
             d_hidden = partial[k] + dqb[k] + dot(d_keys, wt[k, pl.ds(0, kv_width), :])
@@ -528,16 +528,14 @@
             gsum[k] += moment[0:8] + moment[8:16]
             d_inputs = inverse * (d_hidden * gf[k, 0:1, :] - normed * mean)
             go[k, rows, :] = (gb[k, rows, :].astype(F32) + d_inputs).astype(BF16)
-            if k == 0:
+            if k == 1:
 
                 @pl.when(first)
                 def _():
                     send_parts()
 
-            if k < 2:
-                send_grads([k])
-            elif k == KV_HEADS - 1:
-                send_grads([k - 1, k])
+            if k % 2 == 1:
+                send_grads(k // 2)
 
         @pl.when(sec > 0)
         def _():
@@ -594,7 +592,7 @@
         part = pl.ds(pl.multiple_of(peer_y * block, block), block)
         total = wacc[part, :] + dot(ht[0, part, :], d_kv)
         if jy == 0:
-            out_w[:, pl.ds(pl.multiple_of(y * cols, cols), cols)] = total
+            out_w[:, pl.ds(pl.multiple_of(y * cols, cols), cols)] = total.astype(BF16)
         else:
             eo[jy] = total.astype(BF16)
             to_peer(
@@ -619,7 +617,7 @@
     for jy in range(1, grid_y):
         wait_for(eg.at[jy], e_recv.at[jy])
         source_y = (y + grid_y - jy) % grid_y
-        out_w[:, pl.ds(pl.multiple_of(source_y * cols, cols), cols)] = eg[jy].astype(F32)
+        out_w[:, pl.ds(pl.multiple_of(source_y * cols, cols), cols)] = eg[jy]
 
     if grid_y > 1:
         wait_for(eo.at[pl.ds(1, grid_y - 1)], e_send)
@@ -654,7 +652,7 @@
     grad_weight, grad_gain = pl.pallas_call(
         functools.partial(kernel, n_sec, n_dp),
         out_shape=(
-            jax.ShapeDtypeStruct((block, kv2), F32),
+            jax.ShapeDtypeStruct((block, kv2), BF16),
             jax.ShapeDtypeStruct((1, block), F32),
         ),
         in_specs=[any_spec, any_spec, vmem, any_spec, smem, smem, vmem],
@@ -690,9 +688,9 @@
             dma((KV_HEADS,)),
             dma((KV_HEADS,)),
             dma,
-            dma((pieces, KV_HEADS)),
+            dma((pieces, KV_HEADS // 2)),
             dma,
-            dma((pieces, KV_HEADS)),
+            dma((pieces, KV_HEADS // 2)),
             dma,
             dma,
             dma((2,)),
@@ -714,7 +712,7 @@
         ),
         name="relay",
     )(tokens, upstream, gains, w_kv, doc_lengths, seg_lengths, block_mask.transpose(1, 0, 2))
-    return grad_weight[None], grad_gain
+    return grad_weight.astype(F32)[None], grad_gain
 
 
 def solution(mesh):

time: 190 us -> 190 us (level)
  local copies, waits for them, and re-layouts: 2.87 us -> 0.57 us
  other arithmetic: 0 us -> 2.13 us
    unnamed x4 -> x3, local copies, waits for them, and re-layouts: 2.87 us -> 0.57 us
    broadcast_in_dim x0 -> x1, other arithmetic: none -> 2.13 us  [local(): return (grad_weight.astype(F32)[None], grad_gain)]
where the time goes in v7:
time: 190 us
  Pallas kernels  187 us (98%)
  other arithmetic  2.13 us (1%)
    pallas_call x1, Pallas kernels, local(): pl.pallas_call(functools.partial(kernel, n_sec, n_dp), out_shape=(jax.Sha...  187 us

profile of v7, /device:TPU:2, one launch (start us, length us, event | category | flops | bytes accessed | tf_op | source)
XLA Modules:
  0.0 189.9 jit_solution(11510823335387905191)
XLA Ops:
  0.6 186.5 %relay.1 = (bf16[256,1024]{1,0:T(8,128)(2,1)}, f32[1,256]{1,0:T(1,128)}) custom-call(bf16[1,192,4096]{2,1,0:T(8,128)(2,1)} %tok.1, bf16[1,192,4096]{2,1,0:T(8,128)(2,1)} %ups.1, bf16[1,4096]{1,0:T(2,128)(2,1)} %gain.1, bf16[1,4096,1024]{2,1,0:T(8,128)(2,1)} %w.1, s32[1,4]{1,0:T(1,128)} %docs.1, s32[1,4]{1,0:T(1,128)} %segs.1, s32[12,1,12]{2,1,0:T(1,128)} %bitcast.4), custom_call_target="tpu_custom_call" | custom-call | flops 7000000000 | bytes 12582912 | tf_op jit(solution)/shard_map/relay/pallas_call | solution.py:652
  187.2 0.0 copy-start
  187.2 2.1 %bitcast_convert_fusion = f32[1,256,1024]{2,1,0:T(8,128)} fusion(bf16[256,1024]{1,0:T(8,128)(2,1)} %get-tuple-element.4), kind=kLoop, calls=%fused_computation | loop fusion | flops 262144 | bytes 1572864 | tf_op jit(solution)/shard_map/broadcast_in_dim | solution.py:715
  189.3 0.0 copy-done
  189.3 0.6 copy.10
Async XLA Ops:
  187.2 2.1 %copy-start = (f32[1,256]{1,0:T(1,128)S(1)}, f32[1,256]{1,0:T(1,128)}, u32[]{:S(2)}) copy-start(f32[1,256]{1,0:T(1,128)} %get-tuple-element.9) | copy-start | bytes 3076

commit v8 on v7

--- a/solution.py
+++ b/solution.py
@@ -17,7 +17,7 @@
 EPSILON = 1e-06
 
 T = 16
-SPAN = 4
+GROUPS = ((6, 12), (1, 6), (0, 1))
 WINDOW = 128
 PAD = WINDOW - T
 CHUNK = GROUP * HEAD_DIM
@@ -125,7 +125,6 @@
     grid_y = n_dp // KV_HEADS
     cols = 2 * kv_width // grid_y
     x, y = me // grid_y, me % grid_y
-    span_rows = SPAN * T
     first = sec == 0
     last = sec == n_sec - 1
     early = sec < (n_sec + 3) // 4
@@ -265,24 +264,22 @@
         scaled = []
         squares = jnp.zeros((T, 128), F32)
         for k in range(KV_HEADS):
-            if k % 2 == 0:
-                arrival = pltpu.make_async_remote_copy(
-                    src_ref=xb.at[pl.ds(k, 2), rows],
-                    dst_ref=xb.at[pl.ds(k, 2), rows],
-                    send_sem=f_send,
-                    recv_sem=f_recv.at[p, k // 2],
-                    device_id={"section": sec},
-                    device_id_type=MESH,
-                )
-
-                @pl.when(sec > 0)
-                def _():
-                    arrival.wait_recv()
-
-                @pl.when(early & (p == 0))
-                def _():
-                    w_copies[k].wait()
-                    w_copies[k + 1].wait()
+            arrival = pltpu.make_async_remote_copy(
+                src_ref=xb.at[k, rows],
+                dst_ref=xb.at[k, rows],
+                send_sem=f_send,
+                recv_sem=f_recv.at[p, k],
+                device_id={"section": sec},
+                device_id_type=MESH,
+            )
+
+            @pl.when(sec > 0)
+            def _():
+                arrival.wait_recv()
+
+            @pl.when(early & (p == 0))
+            def _():
+                w_copies[k].wait()
 
             values = xb[k, rows, :].astype(F32)
             squares = squares + fold_lanes(values * values)
@@ -323,12 +320,12 @@
 
         @pl.when(sec < n_sec - 1)
         def _():
-            for i in range(KV_HEADS // 2):
+            for k in range(KV_HEADS):
                 pltpu.make_async_remote_copy(
-                    src_ref=xo.at[pl.ds(2 * i, 2), rows],
-                    dst_ref=xb.at[pl.ds(2 * i, 2), rows],
+                    src_ref=xo.at[k, rows],
+                    dst_ref=xb.at[k, rows],
                     send_sem=f_send,
-                    recv_sem=f_recv.at[p, i],
+                    recv_sem=f_recv.at[p, k],
                     device_id={"section": sec + 1},
                     device_id_type=MESH,
                 ).start()
@@ -389,14 +386,13 @@
             for i in range(2):
                 wait_for(hg.at[2, :, pl.ds(i * half, half)], hr_recv.at[i])
 
-        def part(p, carry):
-            rows = pl.ds(pl.multiple_of(p * span_rows, span_rows), span_rows)
+        for low, high in GROUPS:
+            tokens = (high - low) * T
             for c in range(CHUNK // 256):
-                hidden = hg[:, :, rows, pl.ds(c * 256, 256)].reshape(n_dp * span_rows, 256)
-                ht[p, pl.ds(c * 256, 256), :] = hidden.T
-            return carry
-
-        lax.fori_loop(0, pieces // SPAN, part, 0)
+                hidden = hg[:, :, pl.ds(low * T, tokens), pl.ds(c * 256, 256)]
+                ht[pl.ds(c * 256, 256), pl.ds(n_dp * low * T, n_dp * tokens)] = hidden.reshape(
+                    n_dp * tokens, 256
+                ).T
 
     late = jnp.logical_not(early) & (sec >= n_sec - 3)
     middle = jnp.logical_not(early | late)
@@ -478,36 +474,23 @@
         d_vals = jnp.concatenate(own_vals, axis=1).astype(BF16)
         d_kv = jnp.concatenate([d_keys, d_vals], axis=1)
         for c in range(grid_y):
-            do[p // SPAN, c, pl.ds(pl.multiple_of((p % SPAN) * T, T), T), :] = d_kv[
-                :, c * cols : (c + 1) * cols
-            ]
+            do[c, rows, :] = d_kv[:, c * cols : (c + 1) * cols]
         inner = inner + fold_lanes(d_keys.astype(F32) * kb[own, :].astype(F32))
         inner = inner + fold_lanes(d_vals.astype(F32) * vb[own, :].astype(F32))
         mean = jnp.sum(inner, -1, keepdims=True) / width
         inverse = rb[rows, :][:, :1]
 
-        def send_d_kv(part):
-            q = p // SPAN
-            dg[q, 0, part] = do[q, y, part]
-            for j, dp, peer_x, peer_y in peers[1:]:
-                to_peer(
-                    dp, do.at[q, peer_y, part], dg.at[q, j, part], d_send, d_recv.at[q]
-                ).start()
-
         def send_parts():
-            near = sec < 2
-
-            @pl.when((p % SPAN == 0) & jnp.logical_not(near & (p == 0)))
-            def _():
-                send_d_kv(pl.ds(0, span_rows))
-
-            @pl.when(near & (p == 1))
-            def _():
-                send_d_kv(pl.ds(T, span_rows - T))
-
-            @pl.when(near & (p == 0))
-            def _():
-                send_d_kv(pl.ds(0, T))
+            for g, (low, high) in enumerate(GROUPS):
+                part = pl.ds(low * T, (high - low) * T)
+
+                @pl.when(p == low)
+                def _():
+                    dg[0, part] = do[y, part]
+                    for j, dp, peer_x, peer_y in peers[1:]:
+                        to_peer(
+                            dp, do.at[peer_y, part], dg.at[j, part], d_send, d_recv.at[g]
+                        ).start()
 
         def send_grads(pair):
             @pl.when(sec > 0)
@@ -574,23 +557,23 @@
     def _():
         transpose_h()
 
-    def multiply(step, carry):
-        p = pieces // SPAN - 1 - step
-        wait_for(dg.at[p, others], d_recv.at[p])
-        d_kv = dg[p].reshape(n_dp * span_rows, cols)
-        for c in range(CHUNK // 256):
-            part = pl.ds(c * 256, 256)
-            product = dot(ht[p, part, :], d_kv)
-            wacc[part, :] = product + jnp.where(step > 0, wacc[part, :], 0.0)
-        return carry
-
-    lax.fori_loop(0, pieces // SPAN - 1, multiply, 0)
-    wait_for(dg.at[0, others], d_recv.at[0])
-    d_kv = dg[0].reshape(n_dp * span_rows, cols)
-    for jy in list(range(1, grid_y)) + [0]:
+    def product(g, part):
+        low, high = GROUPS[g]
+        tokens = (high - low) * T
+        d_kv = dg[:, pl.ds(low * T, tokens), :].reshape(n_dp * tokens, cols)
+        return dot(ht[part, pl.ds(n_dp * low * T, n_dp * tokens)], d_kv)
+
+    final = len(GROUPS) - 1
+    for g, (low, high) in enumerate(GROUPS):
+        wait_for(dg.at[others, pl.ds(low * T, (high - low) * T)], d_recv.at[g])
+        if g < final:
+            for c in range(CHUNK // 256):
+                part = pl.ds(c * 256, 256)
+                wacc[part, :] = product(g, part) + (wacc[part, :] if g > 0 else 0.0)
+    for jy in (2, 1, 3, 0) if grid_y == 4 else (0,):
         peer_y = (y + jy) % grid_y
         part = pl.ds(pl.multiple_of(peer_y * block, block), block)
-        total = wacc[part, :] + dot(ht[0, part, :], d_kv)
+        total = wacc[part, :] + product(final, part)
         if jy == 0:
             out_w[:, pl.ds(pl.multiple_of(y * cols, cols), cols)] = total.astype(BF16)
         else:
@@ -625,7 +608,7 @@
             wait_for(hg.at[0], hy_send.at[i])
             wait_for(hg.at[2, :, pl.ds(i * half, half)], hr_send.at[i])
     wait_for(hg.at[0, pl.ds(1, KV_HEADS - 1)], hx_send)
-    wait_for(dg.at[:, others], d_send)
+    wait_for(dg.at[others], d_send)
     wait_for(gg.at[others], s_send)
 
     @pl.when(sec < n_sec - 1)
@@ -678,9 +661,9 @@
             pltpu.VMEM((KV_HEADS, 8, CHUNK), F32),
             pltpu.VMEM((KV_HEADS, 8, CHUNK), F32),
             pltpu.VMEM((grid_y, KV_HEADS, seq_len, CHUNK), BF16),
-            pltpu.VMEM((pieces // SPAN, CHUNK, n_dp * SPAN * T), BF16),
-            pltpu.VMEM((pieces // SPAN, grid_y, SPAN * T, cols), BF16),
-            pltpu.VMEM((pieces // SPAN, n_dp, SPAN * T, cols), BF16),
+            pltpu.VMEM((CHUNK, n_dp * seq_len), BF16),
+            pltpu.VMEM((grid_y, seq_len, cols), BF16),
+            pltpu.VMEM((n_dp, seq_len, cols), BF16),
             pltpu.VMEM((CHUNK, cols), F32),
             pltpu.VMEM((grid_y, block, cols), BF16),
             pltpu.VMEM((grid_y, block, cols), BF16),
@@ -688,7 +671,7 @@
             dma((KV_HEADS,)),
             dma((KV_HEADS,)),
             dma,
-            dma((pieces, KV_HEADS // 2)),
+            dma((pieces, KV_HEADS)),
             dma,
             dma((pieces, KV_HEADS // 2)),
             dma,
@@ -698,7 +681,7 @@
             dma((2,)),
             dma((2,)),
             dma,
-            dma((pieces // SPAN,)),
+            dma((len(GROUPS),)),
             dma,
             dma((grid_y,)),
             dma,

time: 190 us -> 191 us (level)
  no operation moved by 1% of the time
where the time goes in v8:
time: 191 us
  Pallas kernels  188 us (98%)
  other arithmetic  2.13 us (1%)
    pallas_call x1, Pallas kernels, local(): pl.pallas_call(functools.partial(kernel, n_sec, n_dp), out_shape=(jax.Sha...  188 us

profile of v8, /device:TPU:2, one launch (start us, length us, event | category | flops | bytes accessed | tf_op | source)
XLA Modules:
  0.0 190.9 jit_solution(10762134395912685815)
XLA Ops:
  0.6 187.6 %relay.1 = (bf16[256,1024]{1,0:T(8,128)(2,1)}, f32[1,256]{1,0:T(1,128)}) custom-call(bf16[1,192,4096]{2,1,0:T(8,128)(2,1)} %tok.1, bf16[1,192,4096]{2,1,0:T(8,128)(2,1)} %ups.1, bf16[1,4096]{1,0:T(2,128)(2,1)} %gain.1, bf16[1,4096,1024]{2,1,0:T(8,128)(2,1)} %w.1, s32[1,4]{1,0:T(1,128)} %docs.1, s32[1,4]{1,0:T(1,128)} %segs.1, s32[12,1,12]{2,1,0:T(1,128)} %bitcast.4), custom_call_target="tpu_custom_call" | custom-call | flops 7000000000 | bytes 12582912 | tf_op jit(solution)/shard_map/relay/pallas_call | solution.py:635
  188.2 0.0 copy-start
  188.2 2.1 %bitcast_convert_fusion = f32[1,256,1024]{2,1,0:T(8,128)} fusion(bf16[256,1024]{1,0:T(8,128)(2,1)} %get-tuple-element.4), kind=kLoop, calls=%fused_computation | loop fusion | flops 262144 | bytes 1572864 | tf_op jit(solution)/shard_map/broadcast_in_dim | solution.py:698
  190.4 0.0 copy-done
  190.4 0.6 copy.10
Async XLA Ops:
  188.2 2.1 %copy-start = (f32[1,256]{1,0:T(1,128)S(1)}, f32[1,256]{1,0:T(1,128)}, u32[]{:S(2)}) copy-start(f32[1,256]{1,0:T(1,128)} %get-tuple-element.9) | copy-start | bytes 3076

commit v9 on v8

--- a/solution.py
+++ b/solution.py
@@ -17,7 +17,7 @@
 EPSILON = 1e-06
 
 T = 16
-GROUPS = ((6, 12), (1, 6), (0, 1))
+GROUPS = ((6, 12), (3, 6), (0, 3))
 WINDOW = 128
 PAD = WINDOW - T
 CHUNK = GROUP * HEAD_DIM
@@ -481,10 +481,18 @@
         inverse = rb[rows, :][:, :1]
 
         def send_parts():
-            for g, (low, high) in enumerate(GROUPS):
+            near = sec < 2
+            whole = [(g, low, high, p == low) for g, (low, high) in enumerate(GROUPS)]
+            g, low, high, here = whole.pop()
+            sends = whole + [
+                (g, low, high, here & jnp.logical_not(near)),
+                (g, low + 1, high, near & (p == low + 1)),
+                (g, low, low + 1, near & here),
+            ]
+            for g, low, high, here in sends:
                 part = pl.ds(low * T, (high - low) * T)
 
-                @pl.when(p == low)
+                @pl.when(here)
                 def _():
                     dg[0, part] = do[y, part]
                     for j, dp, peer_x, peer_y in peers[1:]:

time: 191 us -> 190 us (level)
  Pallas kernels: 188 us -> 186 us
where the time goes in v9:
time: 190 us
  Pallas kernels  186 us (98%)
  other arithmetic  2.13 us (1%)
    pallas_call x1, Pallas kernels, local(): pl.pallas_call(functools.partial(kernel, n_sec, n_dp), out_shape=(jax.Sha...  186 us

profile of v9, /device:TPU:2, one launch (start us, length us, event | category | flops | bytes accessed | tf_op | source)
XLA Modules:
  0.0 189.7 jit_solution(7699383320220382221)
XLA Ops:
  0.6 186.3 %relay.1 = (bf16[256,1024]{1,0:T(8,128)(2,1)}, f32[1,256]{1,0:T(1,128)}) custom-call(bf16[1,192,4096]{2,1,0:T(8,128)(2,1)} %tok.1, bf16[1,192,4096]{2,1,0:T(8,128)(2,1)} %ups.1, bf16[1,4096]{1,0:T(2,128)(2,1)} %gain.1, bf16[1,4096,1024]{2,1,0:T(8,128)(2,1)} %w.1, s32[1,4]{1,0:T(1,128)} %docs.1, s32[1,4]{1,0:T(1,128)} %segs.1, s32[12,1,12]{2,1,0:T(1,128)} %bitcast.4), custom_call_target="tpu_custom_call" | custom-call | flops 7000000000 | bytes 12582912 | tf_op jit(solution)/shard_map/relay/pallas_call | solution.py:643
  187.0 0.0 copy-start
  187.0 2.1 %bitcast_convert_fusion = f32[1,256,1024]{2,1,0:T(8,128)} fusion(bf16[256,1024]{1,0:T(8,128)(2,1)} %get-tuple-element.4), kind=kLoop, calls=%fused_computation | loop fusion | flops 262144 | bytes 1572864 | tf_op jit(solution)/shard_map/broadcast_in_dim | solution.py:706
  189.1 0.0 copy-done
  189.1 0.6 copy.10
Async XLA Ops:
  187.0 2.1 %copy-start = (f32[1,256]{1,0:T(1,128)S(1)}, f32[1,256]{1,0:T(1,128)}, u32[]{:S(2)}) copy-start(f32[1,256]{1,0:T(1,128)} %get-tuple-element.9) | copy-start | bytes 3076

commit v10 on v9

--- a/solution.py
+++ b/solution.py
@@ -354,6 +354,12 @@
             peers.append((jy * KV_HEADS + jx, peer_x * grid_y + peer_y, peer_x, peer_y))
     others = pl.ds(1, n_dp - 1)
 
+    def hops(peer):
+        jx, jy = peer[0] % KV_HEADS, peer[0] // KV_HEADS
+        return min(jx, KV_HEADS - jx) + min(jy, grid_y - jy)
+
+    far_first = sorted(peers[1:], key=hops, reverse=True)
+
     upper, lower = x * grid_y + (y + 1) % grid_y, x * grid_y + (y + grid_y - 1) % grid_y
     half = seq_len // 2
     far = grid_y - 1
@@ -495,7 +501,7 @@
                 @pl.when(here)
                 def _():
                     dg[0, part] = do[y, part]
-                    for j, dp, peer_x, peer_y in peers[1:]:
+                    for j, dp, peer_x, peer_y in far_first:
                         to_peer(
                             dp, do.at[peer_y, part], dg.at[j, part], d_send, d_recv.at[g]
                         ).start()

time: 190 us -> 190 us (level)
  no operation moved by 1% of the time
where the time goes in v10:
time: 190 us; the launch traced here: 189 us
  Pallas kernels  186 us (98%)
  other arithmetic  2.13 us (1%)
    pallas_call x1, Pallas kernels, local(): pl.pallas_call(functools.partial(kernel, n_sec, n_dp), out_shape=(jax.Sha...  186 us

profile of v10, /device:TPU:2, one launch (start us, length us, event | category | flops | bytes accessed | tf_op | source)
XLA Modules:
  0.0 189.3 jit_solution(483757208028815597)
XLA Ops:
  0.6 186.0 %relay.1 = (bf16[256,1024]{1,0:T(8,128)(2,1)}, f32[1,256]{1,0:T(1,128)}) custom-call(bf16[1,192,4096]{2,1,0:T(8,128)(2,1)} %tok.1, bf16[1,192,4096]{2,1,0:T(8,128)(2,1)} %ups.1, bf16[1,4096]{1,0:T(2,128)(2,1)} %gain.1, bf16[1,4096,1024]{2,1,0:T(8,128)(2,1)} %w.1, s32[1,4]{1,0:T(1,128)} %docs.1, s32[1,4]{1,0:T(1,128)} %segs.1, s32[12,1,12]{2,1,0:T(1,128)} %bitcast.4), custom_call_target="tpu_custom_call" | custom-call | flops 7000000000 | bytes 12582912 | tf_op jit(solution)/shard_map/relay/pallas_call | solution.py:649
  186.6 0.0 copy-start
  186.6 2.1 %bitcast_convert_fusion = f32[1,256,1024]{2,1,0:T(8,128)} fusion(bf16[256,1024]{1,0:T(8,128)(2,1)} %get-tuple-element.4), kind=kLoop, calls=%fused_computation | loop fusion | flops 262144 | bytes 1572864 | tf_op jit(solution)/shard_map/broadcast_in_dim | solution.py:712
  188.7 0.0 copy-done
  188.7 0.6 copy.10
Async XLA Ops:
  186.6 2.1 %copy-start = (f32[1,256]{1,0:T(1,128)S(1)}, f32[1,256]{1,0:T(1,128)}, u32[]{:S(2)}) copy-start(f32[1,256]{1,0:T(1,128)} %get-tuple-element.9) | copy-start | bytes 3076
